TPU v7x, 32 devices: a whole 2x2x4 slice. The times are simulated.
32 devices in a mesh: grp: 2 (over y), row: 4 (over z), col: 2 (over x), sub: 2 (over core).
Axes of the slice: x: 2, y: 2, z: 4, core: 2. Of those that a mesh axis runs over, the one named last changes fastest.
Arguments:
- fine_field: bfloat16 [64, 512, 1024], P(('grp', 'row'), None, ('col', 'sub')), parts along dimension 0, may hold values from -6 to 6
- conv_taps: bfloat16 [3, 3, 1024], P(None, None, ('col', 'sub')), may hold values from -1 to 1
- position_table: bfloat16 [256, 1024], P(None, ('col', 'sub')), may hold values from -3 to 3
- coarse_bands: bfloat16 [8, 34, 64], P(('grp', 'row')), parts along dimension 0, may hold values from -6 to 6
- band_weight: bfloat16 [34, 2048], replicated, may hold values from -3 to 3
- noise_step: int32 [1], replicated, may hold values from 0 to 17
- land_tiles: int32 [64, 4], P(('grp', 'row')), parts along dimension 0, may hold values from 0 to 1, as said below
- tile_owner: int32 [64, 4], P(('grp', 'row')), parts along dimension 0, may hold values from 0 to 3, as said below
- neighbour_lists: int32 [64, 4, 128], P(('grp', 'row')), parts along dimension 0, may hold values from 0 to 511
- tile_order: int32 [64, 4, 128], P(('grp', 'row')), parts along dimension 0, may hold values from 0 to 127, each once within a row
- expert_projections: bfloat16 [4, 1024, 3, 1024], P('row', None, None, ('col', 'sub'))
- expert_output: bfloat16 [4, 1024, 1024], P('row', ('col', 'sub')), may hold values from -0.1875 to 0.1875
Outputs:
- denoised: bfloat16 [64, 512, 1024], P(('grp', 'row'), None, ('col', 'sub')), parts along dimension 0
There are 2 independent parts, one for each index of `grp`. A program takes and returns all parts, laid end to end along the dimension named above; an argument that names none is the same for every part. Nothing has to cross between parts.
Inputs may be any that keep to these rules, and one draw needn't show every extreme that they name: `land_tiles`: every strip (the 8 latitude rows that one index of row holds) has 8 or more land tiles. `tile_owner`: of the land tiles of one strip at most 8 have the same owner; in every draw some owner has exactly 8 land tiles of every strip.
All inputs are finite; a program needn't handle non-finite values.
Results may differ from a plain program's by a relative error of at most 0.0087.
Values may be sent and summed in bfloat16 or wider, within the bound.
A program may use at most 128 MiB of HBM per device.

v0:
```python
import math

import jax
import jax.numpy as jnp
from jax import lax
from jax.sharding import PartitionSpec as P

HEAD = 64
TILE = 128


EPSILON = 1e-05


def extended(cells, sides, width):
    for axis, dim in sides:
        count = lax.axis_size(axis)
        ends = count - 1
        head = lax.slice_in_dim(cells, 0, width, axis=dim)
        tail = lax.slice_in_dim(cells, cells.shape[dim] - width, cells.shape[dim], axis=dim)
        cells = jnp.concatenate(
            [
                lax.ppermute(tail, axis, [(i, (i + 1) % count) for i in range(ends)]),
                cells,
                lax.ppermute(head, axis, [((i + 1) % count, i) for i in range(ends)]),
            ],
            axis=dim,
        )
    return cells


def step_embedding(noise_step, emb_width):
    positions = jnp.arange(emb_width, dtype=jnp.float32)
    frequency = jnp.exp(-4.0 * positions / emb_width)
    return 0.5 * jnp.sin((noise_step[0].astype(jnp.float32) + 1.0) * frequency)


def attend_block(inputs, scale_rows, shift_rows, projection, out_weight):
    values = inputs.astype(jnp.float32)
    average = jnp.mean(values, axis=-1, keepdims=True)
    centred = values - average
    variance = jnp.mean(centred * centred, axis=-1, keepdims=True)
    normed = centred * lax.rsqrt(variance + EPSILON)
    hidden = (normed * (1.0 + scale_rows[:, None, :]) + shift_rows[:, None, :]).astype(jnp.bfloat16)
    slot_count = inputs.shape[0]
    widths = projection.shape[2]
    head_count = widths // HEAD
    queries = jnp.einsum(
        "sqd,dw->sqw", hidden[:, :TILE], projection[:, 0], preferred_element_type=jnp.float32
    ).astype(jnp.bfloat16)
    key_values = jnp.einsum(
        "skd,dtw->sktw", hidden, projection[:, 1:], preferred_element_type=jnp.float32
    ).astype(jnp.bfloat16)
    query_heads = queries.reshape(slot_count, TILE, head_count, HEAD)
    key_heads = key_values[:, :, 0].reshape(slot_count, -1, head_count, HEAD)
    value_heads = key_values[:, :, 1].reshape(slot_count, -1, head_count, HEAD)
    scores = jnp.einsum(
        "sqhe,skhe->shqk", query_heads, key_heads, preferred_element_type=jnp.float32
    ) * (1.0 / math.sqrt(HEAD))
    highest = jnp.max(scores, axis=-1, keepdims=True)
    weights = jnp.exp(scores - highest)
    chances = (weights / jnp.sum(weights, axis=-1, keepdims=True)).astype(jnp.bfloat16)
    mixture = jnp.einsum(
        "shqk,skhe->sqhe", chances, value_heads, preferred_element_type=jnp.float32
    ).astype(jnp.bfloat16)
    mixture = mixture.reshape(slot_count, TILE, widths)
    return jnp.einsum("sqw,wd->sqd", mixture, out_weight, preferred_element_type=jnp.float32)


def pick_rows(mod_table, first_slot, slot_total, per_source):
    sources = (first_slot + jnp.arange(slot_total, dtype=jnp.int32)) // per_source
    select = (sources[:, None] == jnp.arange(mod_table.shape[0], dtype=jnp.int32)[None, :]).astype(
        jnp.float32
    )
    return jnp.dot(select, mod_table, precision=lax.Precision.HIGHEST)


def body(
    fine_field,
    conv_taps,
    position_table,
    coarse_bands,
    band_weight,
    noise_step,
    land_tiles,
    tile_owner,
    neighbour_lists,
    tile_order,
    expert_projections,
    expert_output,
):
    lat_rows, lon_cells, channels = fine_field.shape
    tiles_row = land_tiles.shape[1]
    tile_count = lat_rows * tiles_row
    strips = lax.axis_size("row")
    per_owner = tile_count // strips
    padded = extended(fine_field, (("row", 0),), 1)
    padded = jnp.pad(padded, ((0, 0), (1, 1), (0, 0)))
    tap_values = conv_taps.astype(jnp.float32)
    running = fine_field.astype(jnp.float32)
    for row_shift in range(3):
        for col_shift in range(3):
            running = running + tap_values[row_shift, col_shift] * padded[
                row_shift : row_shift + lat_rows, col_shift : col_shift + lon_cells
            ].astype(jnp.float32)
    smoothed = running.astype(jnp.bfloat16)
    land_flat = land_tiles.reshape(tile_count)
    owner_flat = tile_owner.reshape(tile_count)
    tile_ids = jnp.arange(tile_count, dtype=jnp.int32)
    earlier = (
        (owner_flat[None, :] == owner_flat[:, None])
        & (land_flat[None, :] > 0)
        & (tile_ids[None, :] < tile_ids[:, None])
    )
    slot_rank = jnp.sum(earlier.astype(jnp.int32), axis=1)
    slot_of = owner_flat * per_owner + slot_rank
    chosen = ((slot_of[None, :] == tile_ids[:, None]) & (land_flat[None, :] > 0)).astype(jnp.int32)
    tile_of = jnp.sum(chosen * tile_ids[None, :], axis=1)
    occupied = jnp.sum(chosen, axis=1)
    lat_of = tile_of // tiles_row
    col_of = tile_of % tiles_row
    order_rows = tile_order.reshape(tile_count, TILE)[tile_of]
    near_rows = neighbour_lists.reshape(tile_count, TILE)[tile_of]
    query_cells = lat_of[:, None] * lon_cells + col_of[:, None] * TILE + order_rows
    near_cells = lat_of[:, None] * lon_cells + near_rows
    cell_index = jnp.concatenate([query_cells, near_cells], axis=1)
    flat_field = smoothed.reshape(lat_rows * lon_cells, channels)
    sequence = (
        jnp.take(flat_field, cell_index, axis=0).astype(jnp.float32)
        + position_table.astype(jnp.float32)[None]
    ).astype(jnp.bfloat16)
    outgoing = sequence.reshape(strips, per_owner, 2 * TILE, channels)
    arrived = lax.all_to_all(outgoing, "row", split_axis=0, concat_axis=0, tiled=True)
    arrived = arrived.reshape(tile_count, 2 * TILE, 1, channels)
    gathered_bands = lax.all_gather(coarse_bands, "row", axis=0, tiled=True)
    band_means = jnp.mean(gathered_bands.astype(jnp.float32), axis=2)
    modulation = jnp.dot(
        band_means, band_weight.astype(jnp.float32), precision=lax.Precision.HIGHEST
    ) + step_embedding(noise_step, band_weight.shape[1])
    full_width = band_weight.shape[1] // 2
    group_size = lax.axis_size(("col", "sub"))
    my_slots = tile_count // group_size
    spread = lax.all_to_all(arrived, ("col", "sub"), split_axis=0, concat_axis=2, tiled=True)
    inputs = spread.reshape(my_slots, 2 * TILE, full_width)
    full_proj, full_out = (
        lax.all_gather(expert_projections, ("col", "sub"), axis=3, tiled=True),
        lax.all_gather(expert_output, ("col", "sub"), axis=1, tiled=True),
    )
    local_mod = pick_rows(
        modulation, lax.axis_index(("col", "sub")) * my_slots, my_slots, per_owner
    )
    heads_out = attend_block(
        inputs, local_mod[:, :full_width], local_mod[:, full_width:], full_proj[0], full_out[0]
    ).astype(jnp.bfloat16)
    returned = lax.all_to_all(
        heads_out.reshape(my_slots, TILE, group_size, channels),
        ("col", "sub"),
        split_axis=2,
        concat_axis=0,
        tiled=True,
    )
    returned = returned.reshape(strips, per_owner, TILE, channels)
    results = lax.all_to_all(returned, "row", split_axis=0, concat_axis=0, tiled=True)
    update = results.reshape(tile_count, TILE, channels).astype(jnp.float32) * occupied[
        :, None, None
    ].astype(jnp.float32)
    merged = (
        flat_field.astype(jnp.float32).at[query_cells.reshape(-1)].add(update.reshape(-1, channels))
    )
    return merged.astype(jnp.bfloat16).reshape(lat_rows, lon_cells, channels)


def solution(mesh):
    placed = (
        P(("grp", "row"), None, ("col", "sub")),
        P(None, None, ("col", "sub")),
        P(None, ("col", "sub")),
        P(("grp", "row"), None, None),
        P(),
        P(),
        P(("grp", "row"), None),
        P(("grp", "row"), None),
        P(("grp", "row"), None, None),
        P(("grp", "row"), None, None),
        P("row", None, None, ("col", "sub")),
        P("row", ("col", "sub"), None),
    )
    return jax.shard_map(
        body,
        mesh=mesh,
        in_specs=placed,
        out_specs=P(("grp", "row"), None, ("col", "sub")),
        check_vma=False,
    )
```

profile of v0, /device:TPU:0, one launch (start us, length us, event | category | flops | bytes accessed | tf_op | source)
XLA Modules:
  0.0 452.9 jit_solution(8113199860776294310)
XLA Ops:
  8.5 4.9 %collective-permute-start = (bf16[1,512,256]{2,1,0:T(8,128)(2,1)}, bf16[1,512,256]{2,1,0:T(8,128)(2,1)S(1)}, u32[]{:S(2)}, u32[]{:S(2)}) collective-permute-start(bf16[1,512,256]{2,1,0:T(8,128)(2,1)} %get-tuple-element.13), channel_id=1, source_target_pairs={{0,4},{4,8},{8,12},{1,5},{5,9},{9,13},{2,6},{6,10},{10,14},{3,7},{... | collective-permute-start | bytes 786440 | tf_op jit(solution)/shard_map/ppermute | solution.py:23
  24.0 4.3 fusion.15
  28.3 33.1 %gather_fusion.2 = bf16[8192,256]{1,0:T(8,128)(2,1)} fusion(bf16[4096,256]{1,0:T(8,128)(2,1)S(1)} %bitcast.95, s32[8192]{0:T(1024)S(1)} %broadcast_clamp_fusion), kind=kCustom, calls=%fused_computation.2 | custom fusion | bytes 8421376 | tf_op jit(solution)/shard_map/jit(_take)/gather | solution.py:129
  61.4 3.9 add_convert_fusion.1
  65.3 97.2 %all_to_all.34 = bf16[4,8,256,256]{3,2,1,0:T(8,128)(2,1)} all-to-all(bf16[4,8,256,256]{3,2,1,0:T(8,128)(2,1)S(1)} %add_convert_fusion.1), channel_id=1, replica_groups=mesh['grp'=2,'row'=4,'col'=2,'sub'=2] {'row'}, dimensions={0} | all-to-all | bytes 8388608 | tf_op jit(solution)/shard_map/all_to_all | solution.py:133
  162.5 5.0 %all-to-all-start.1 = ((bf16[32,256,1,256]{3,1,2,0:T(8,128)(2,1)}), bf16[32,256,1,256]{3,1,2,0:T(8,128)(2,1)}, u32[]{:S(2)}, u32[]{:S(2)}) async-start(bf16[32,256,1,256]{3,1,2,0:T(8,128)(2,1)} %bitcast.96), calls=%async_computation.1 | async-start | bytes 8388608 | tf_op jit(solution)/shard_map/all_to_all | solution.py:143
  168.9 13.1 %all_gather.9 = bf16[4,34,64]{2,1,0:T(8,128)(2,1)S(1)} all-gather(bf16[1,34,64]{2,1,0:T(8,128)(2,1)S(1)} %copy-done.5), channel_id=1, replica_groups=mesh['grp'=2,'row'=4,'col'=2,'sub'=2] {'row'}, dimensions={0}, use_global_device_ids=true | all-gather | bytes 21760 | tf_op jit(solution)/shard_map/all_gather | solution.py:135
  182.7 44.3 %all-to-all-done.1 = bf16[32,256,1,256]{3,1,2,0:T(8,128)(2,1)} async-done(((bf16[32,256,1,256]{3,1,2,0:T(8,128)(2,1)}), bf16[32,256,1,256]{3,1,2,0:T(8,128)(2,1)}, u32[]{:S(2)}, u32[]{:S(2)}) %all-to-all-start.1) | async-done | bytes 4194336 | tf_op jit(solution)/shard_map/all_to_all | solution.py:143
  227.0 6.5 %convert_bitcast_fusion = f32[8,256,4,1,256]{4,1,0,2,3:T(8,128)} fusion(bf16[4,8,256,1,256]{4,2,1,0,3:T(8,128)(2,1)} %bitcast.25), kind=kLoop, calls=%fused_computation.9 | loop fusion | flops 2097152 | bytes 12582912 | tf_op jit(solution)/shard_map/convert_element_type | solution.py:39
  236.3 12.0 %copy.40 = f32[8,256,4,1,256]{4,2,1,0,3:T(4,128)} copy(f32[8,256,4,1,256]{4,1,0,2,3:T(8,128)} %convert_bitcast_fusion) | data formatting | bytes 16777216 | tf_op jit(solution)/shard_map/convert_element_type | solution.py:39
  248.2 10.7 %reshape.368 = f32[8,256,1024]{2,1,0:T(8,128)} reshape(f32[8,256,4,1,256]{4,2,1,0,3:T(4,128)} %copy.40) | data formatting | bytes 16777216 | tf_op jit(solution)/shard_map/convert_element_type | solution.py:39
  262.0 5.6 %add_convert_fusion = bf16[8,256,1024]{2,1,0:T(8,128)(2,1)} fusion(f32[8,256,1024]{2,1,0:T(8,128)} %reshape.368, f32[8,1024]{1,0:T(8,128)S(1)} %get-tuple-element.16, f32[8,1024]{1,0:T(8,128)S(1)} %get-tuple-element.15, f32[8,256]{1,0:T(8,128)S(1)} %add_rsqrt_fusion, f32[8,256]{1,0:T(8,128)S(1)} %broadcast_multiply_fusion), kind=kLoop, calls=%fused_computation.11 | loop fusion | flops 10485760 | bytes 12664832 | tf_op jit(solution)/shard_map/convert_element_type | solution.py:44
  267.6 12.1 %convolution_convert_fusion = bf16[8,256,2,1024]{3,1,2,0:T(8,128)(2,1)S(1)} fusion(bf16[1024,3,1024]{2,0,1:T(8,128)(2,1)} %bitcast.118, bf16[8,256,1024]{2,1,0:T(8,128)(2,1)} %add_convert_fusion), kind=kOutput, calls=%fused_computation.17 | convolution fusion | flops 8594128896 | bytes 16777216 | tf_op jit(solution)/shard_map/skd,dtw->sktw/dot_general | solution.py:51
  279.7 5.3 %fusion.34 = bf16[8,128,1024]{2,1,0:T(8,128)(2,1)} fusion(bf16[1024,3,1024]{2,0,1:T(8,128)(2,1)} %bitcast.119, bf16[8,256,1024]{2,1,0:T(8,128)(2,1)S(1)} %copy-done.4), kind=kOutput, calls=%fused_computation.52 | convolution fusion | flops 2148532224 | bytes 6291456 | tf_op jit(solution)/shard_map/sqd,dw->sqw/dot_general | solution.py:48
  288.7 6.5 %copy.43 = bf16[8,256,1,1024]{1,3,0,2:T(8,128)(2,1)} copy(bf16[8,256,1,1024]{3,1,2,0:T(8,128)(2,1)} %get-tuple-element.11) | data formatting | bytes 8388608 | tf_op jit(solution)/shard_map/slice | solution.py:55
  295.1 3.9 copy.42
  299.0 6.5 %copy.41 = bf16[8,256,1,1024]{1,3,0,2:T(8,128)(2,1)} copy(bf16[8,256,1,1024]{3,1,2,0:T(8,128)(2,1)} %get-tuple-element.12) | data formatting | bytes 8388608 | tf_op jit(solution)/shard_map/slice | solution.py:56
  305.5 11.4 %fusion.60 = (f32[8,16,128]{2,1,0:T(8,128)S(1)}, f32[8,16,128,256]{3,2,1,0:T(8,128)}) fusion(bf16[8,128,16,64]{1,3,2,0:T(8,128)(2,1)} %bitcast.101, bf16[8,256,16,64]{1,3,2,0:T(8,128)(2,1)} %bitcast.97), kind=kOutput, calls=%fused_computation.116 | convolution fusion | flops 549454080 | bytes 23134208 | tf_op jit(solution)/shard_map/sub | solution.py:61
  317.0 10.0 %fusion.37 = bf16[8,16,64,128]{3,2,1,0:T(8,128)(2,1)} fusion(bf16[8,256,16,64]{1,3,2,0:T(8,128)(2,1)} %bitcast.102, f32[8,16,128,256]{3,2,1,0:T(8,128)} %get-tuple-element.27, f32[8,16,128]{2,1,0:T(8,128)S(1)} %get-tuple-element.26), kind=kOutput, calls=%fused_computation.53 | convolution fusion | flops 546308096 | bytes 23134208 | tf_op jit(solution)/shard_map/shqk,skhe->sqhe/dot_general | solution.py:63
  327.0 4.6 %fusion.31 = bf16[8,128,1024]{2,1,0:T(8,128)(2,1)S(1)} fusion(bf16[8,128,1024]{1,2,0:T(8,128)(2,1)} %bitcast.120, bf16[1,1024,1024]{2,1,0:T(8,128)(2,1)} %all-gather.5.cloned.1.call-done), kind=kOutput, calls=%fused_computation.51 | convolution fusion | flops 2148532224 | bytes 6291456 | tf_op jit(solution)/shard_map/sqw,wd->sqd/dot_general | solution.py:67
  331.9 28.9 %all_to_all.35 = bf16[8,128,4,256]{3,1,0,2:T(8,128)(2,1)} all-to-all(bf16[8,128,4,256]{3,1,0,2:T(8,128)(2,1)S(1)} %bitcast.100), channel_id=1, replica_groups=mesh['grp'=2,'row'=4,'col'=2,'sub'=2] {'col','sub'}, dimensions={2} | all-to-all | bytes 4194304 | tf_op jit(solution)/shard_map/all_to_all | solution.py:155
  360.8 4.4 all-to-all-start.3
  367.8 45.6 %all-to-all-done.3 = bf16[4,8,128,256]{3,2,1,0:T(8,128)(2,1)} async-done(((bf16[4,8,128,256]{3,2,1,0:T(8,128)(2,1)}), bf16[4,8,128,256]{3,2,1,0:T(8,128)(2,1)}, u32[]{:S(2)}, u32[]{:S(2)}) %all-to-all-start.3) | async-done | bytes 2097184 | tf_op jit(solution)/shard_map/all_to_all | solution.py:163
  413.4 29.0 %scatter_custom_fusion = f32[4096,256]{1,0:T(8,128)} fusion(f32[4096,256]{1,0:T(8,128)} %bitcast_convert_fusion, s32[4096]{0:T(1024)S(1)} %bitcast.108, bf16[4096,256]{1,0:T(8,128)(2,1)} %bitcast.51, f32[4096]{0:T(1024)S(1)} %broadcast_bitcast_fusion), kind=kCustom, calls=%fused_computation.33 | custom fusion | flops 3145728 | bytes 6307840 | tf_op jit(solution)/shard_map/scatter-add | solution.py:168
  (65 shorter events, 29.8 us)
Async XLA Ops:
  6.5 175.7 %copy-start = (bf16[34,2048]{1,0:T(8,128)(2,1)S(1)}, bf16[34,2048]{1,0:T(8,128)(2,1)}, u32[]{:S(2)}) copy-start(bf16[34,2048]{1,0:T(8,128)(2,1)} %param.16) | copy-start | bytes 417796
  6.5 16.5 %copy-start.2 = (bf16[8,512,256]{2,1,0:T(8,128)(2,1)S(1)}, bf16[8,512,256]{2,1,0:T(8,128)(2,1)}, u32[]{:S(2)}) copy-start(bf16[8,512,256]{2,1,0:T(8,128)(2,1)} %param.12) | copy-start | bytes 6291460
  6.5 261.1 %all-gather.3.cloned.1.call-start = ((), (), s32[]{:S(2)}) async-start(), calls=%async_computation.4 | async-start | bytes 7864320 | tf_op jit(solution)/shard_map/all_gather | solution.py:146
  8.5 13.3 %collective-permute-start = (bf16[1,512,256]{2,1,0:T(8,128)(2,1)}, bf16[1,512,256]{2,1,0:T(8,128)(2,1)S(1)}, u32[]{:S(2)}, u32[]{:S(2)}) collective-permute-start(bf16[1,512,256]{2,1,0:T(8,128)(2,1)} %get-tuple-element.13), channel_id=1, source_target_pairs={{0,4},{4,8},{8,12},{1,5},{5,9},{9,13},{2,6},{6,10},{10,14},{3,7},{... | collective-permute-start | bytes 786440 | tf_op jit(solution)/shard_map/ppermute | solution.py:23
  13.4 9.7 %collective-permute-start.1 = (bf16[1,512,256]{2,1,0:T(8,128)(2,1)S(1)}, bf16[1,512,256]{2,1,0:T(8,128)(2,1)S(1)}, u32[]{:S(2)}, u32[]{:S(2)}) collective-permute-start(bf16[1,512,256]{2,1,0:T(8,128)(2,1)S(1)} %get-tuple-element.14), channel_id=1, source_target_pairs={{4,0},{8,4},{12,8},{5,1},{9,5},{13,9},{6,2},{10,6},{14,10},{7,3},{... | collective-permute-start | bytes 786440 | tf_op jit(solution)/shard_map/ppermute | solution.py:25
  20.3 3.7 copy-start.3
  162.5 6.4 %copy-start.5 = (bf16[1,34,64]{2,1,0:T(8,128)(2,1)S(1)}, bf16[1,34,64]{2,1,0:T(8,128)(2,1)}, u32[]{:S(2)}) copy-start(bf16[1,34,64]{2,1,0:T(8,128)(2,1)} %param.15) | copy-start | bytes 13060
  162.5 64.5 %all-to-all-start.1 = ((bf16[32,256,1,256]{3,1,2,0:T(8,128)(2,1)}), bf16[32,256,1,256]{3,1,2,0:T(8,128)(2,1)}, u32[]{:S(2)}, u32[]{:S(2)}) async-start(bf16[32,256,1,256]{3,1,2,0:T(8,128)(2,1)} %bitcast.96), calls=%async_computation.1 | async-start | bytes 8388608 | tf_op jit(solution)/shard_map/all_to_all | solution.py:143
  167.5 159.5 %all-gather.5.cloned.1.call-start = ((), (), s32[]{:S(2)}) async-start(), calls=%async_computation.5 | async-start | bytes 2621440 | tf_op jit(solution)/shard_map/all_gather | solution.py:147
  267.6 12.1 %copy-start.4 = (bf16[8,256,1024]{2,1,0:T(8,128)(2,1)S(1)}, bf16[8,256,1024]{2,1,0:T(8,128)(2,1)}, u32[]{:S(2)}) copy-start(bf16[8,256,1024]{2,1,0:T(8,128)(2,1)} %add_convert_fusion) | copy-start | bytes 12582916
  360.8 52.6 %all-to-all-start.3 = ((bf16[4,8,128,256]{3,2,1,0:T(8,128)(2,1)}), bf16[4,8,128,256]{3,2,1,0:T(8,128)(2,1)}, u32[]{:S(2)}, u32[]{:S(2)}) async-start(bf16[4,8,128,256]{3,2,1,0:T(8,128)(2,1)} %bitcast.99), calls=%async_computation.3 | async-start | bytes 4194304 | tf_op jit(solution)/shard_map/all_to_all | solution.py:163
  413.4 32.7 %copy-start.1 = (bf16[34,2048]{1,0:T(8,128)(2,1)S(1)}, bf16[34,2048]{1,0:T(8,128)(2,1)}, u32[]{:S(2)}) copy-start(bf16[34,2048]{1,0:T(8,128)(2,1)} %param.16) | copy-start | bytes 417796
Sparse Core Ops, SparseCore 0:
  14.8 49.5 all-gather.2
  169.9 33.4 all-gather.4
where the time goes:
time: 454 us; the launch traced here: 453 us
  blocking collectives  139 us (31%)
  waiting for transfers between devices  91.9 us (20%)
  local copies, waits for them, and re-layouts  83.2 us (18%)
  other arithmetic  64.8 us (14%)
  matrix products  43.8 us (10%)
  starting transfers between devices  15.7 us (3%)
  between operations  14.3 us (3%)
    all_to_all x1, blocking collectives, body(): lax.all_to_all(outgoing, 'row', split_axis=0, concat_axis=0, tiled=True)  97.2 us
    all_to_all x1, waiting for transfers between devices, body(): lax.all_to_all(returned, 'row', split_axis=0, concat_axis=0, tiled=True)  45.6 us
    all_to_all x1, waiting for transfers between devices, body(): lax.all_to_all(arrived, ('col', 'sub'), split_axis=0, concat_axis=2, tile...  44.3 us
    gather x1, local copies, waits for them, and re-layouts, body(): jnp.take(flat_field, cell_index, axis=0).astype(jnp.float32)  33.1 us
    scatter-add x1, other arithmetic, body(): flat_field.astype(jnp.float32).at[query_cells.reshape(-1)]  29 us
    all_to_all x1, blocking collectives, body(): lax.all_to_all(heads_out.reshape(my_slots, TILE, group_size, channels), (...  28.9 us
    convert_element_type x2, local copies, waits for them, and re-layouts, attend_block(): values = inputs.astype(jnp.float32)  22.7 us
    all_gather x1, blocking collectives, body(): gathered_bands = lax.all_gather(coarse_bands, 'row', axis=0, tiled=True)  13.1 us
  transfers between devices with their start and end apart: 6, of which 3 were waited for; matrix products, arithmetic and copies ran while one was open for 34% of the time, Pallas kernels for 0%

commit v1 on v0

v1 whole, which is shorter than its diff:
```python
import functools
import math

import jax
import jax.numpy as jnp
from jax import lax
from jax.experimental import pallas as pl
from jax.experimental.pallas import tpu as pltpu
from jax.sharding import PartitionSpec as P

HEAD = 64
TILE = 128


EPSILON = 1e-05


def extended(cells, sides, width):
    for axis, dim in sides:
        count = lax.axis_size(axis)
        ends = count - 1
        head = lax.slice_in_dim(cells, 0, width, axis=dim)
        tail = lax.slice_in_dim(cells, cells.shape[dim] - width, cells.shape[dim], axis=dim)
        cells = jnp.concatenate(
            [
                lax.ppermute(tail, axis, [(i, (i + 1) % count) for i in range(ends)]),
                cells,
                lax.ppermute(head, axis, [((i + 1) % count, i) for i in range(ends)]),
            ],
            axis=dim,
        )
    return cells


def step_embedding(noise_step, emb_width):
    positions = jnp.arange(emb_width, dtype=jnp.float32)
    frequency = jnp.exp(-4.0 * positions / emb_width)
    return 0.5 * jnp.sin((noise_step[0].astype(jnp.float32) + 1.0) * frequency)


def gather_kernel(tile_ref, field_ref, index_ref, table_ref, out_ref):
    tile = tile_ref[pl.program_id(0)]
    table = index_ref[...]
    lanes = lax.broadcasted_iota(jnp.int32, table.shape, 1)
    column = jnp.sum(jnp.where(lanes == tile, table, 0), axis=1, keepdims=True)
    cells = field_ref.shape[1]
    spots = lax.broadcasted_iota(jnp.int32, (table.shape[0], cells), 1)
    select = jnp.where(spots == column, 1.0, 0.0).astype(jnp.bfloat16)
    picked = jnp.dot(select, field_ref[0], preferred_element_type=jnp.float32)
    out_ref[0] = (picked + table_ref[...].astype(jnp.float32)).astype(jnp.bfloat16)


def gather_tiles(smoothed, tile_of, index_table, position_table, tiles_row):
    lat_rows, lon_cells, channels = smoothed.shape
    tokens, tile_count = index_table.shape
    return pl.pallas_call(
        gather_kernel,
        grid_spec=pltpu.PrefetchScalarGridSpec(
            num_scalar_prefetch=1,
            grid=(tile_count,),
            in_specs=[
                pl.BlockSpec((1, lon_cells, channels), lambda s, t: (t[s] // tiles_row, 0, 0)),
                pl.BlockSpec((tokens, tile_count), lambda s, t: (0, 0)),
                pl.BlockSpec((tokens, channels), lambda s, t: (0, 0)),
            ],
            out_specs=pl.BlockSpec((1, tokens, channels), lambda s, t: (s, 0, 0)),
        ),
        out_shape=jax.ShapeDtypeStruct((tile_count, tokens, channels), jnp.bfloat16),
        compiler_params=pltpu.CompilerParams(vmem_limit_bytes=32 * 1024 * 1024),
        cost_estimate=pl.CostEstimate(
            flops=2 * tile_count * tokens * lon_cells * channels,
            bytes_accessed=2 * tile_count * (lon_cells + tokens) * channels,
            transcendentals=0,
        ),
        name="gather_tiles",
    )(tile_of, smoothed, index_table, position_table)


def merge_kernel(tiles_row, slot_ref, land_ref, field_ref, order_ref, *refs):
    out_ref = refs[-1]
    row = pl.program_id(0)
    for col in range(tiles_row):
        span = pl.ds(col * TILE, TILE)
        spots = lax.broadcasted_iota(jnp.int32, (TILE, TILE), 0)
        place = jnp.where(spots == order_ref[0, col : col + 1, :], 1.0, 0.0).astype(jnp.bfloat16)
        moved = jnp.dot(place, refs[col][0], preferred_element_type=jnp.float32)
        kept = field_ref[0, span, :]
        added = (kept.astype(jnp.float32) + moved).astype(jnp.bfloat16)
        is_land = land_ref[row * tiles_row + col] > 0
        out_ref[0, span, :] = jnp.where(is_land, added, kept)


def merge_tiles(smoothed, results, slot_of, land, tile_order):
    lat_rows, lon_cells, channels = smoothed.shape
    tiles_row = tile_order.shape[1]

    def picked(col):
        return pl.BlockSpec(
            (1, TILE, channels), lambda r, s, m: (s[r * tiles_row + col], 0, 0)
        )

    return pl.pallas_call(
        functools.partial(merge_kernel, tiles_row),
        grid_spec=pltpu.PrefetchScalarGridSpec(
            num_scalar_prefetch=2,
            grid=(lat_rows,),
            in_specs=[
                pl.BlockSpec((1, lon_cells, channels), lambda r, s, m: (r, 0, 0)),
                pl.BlockSpec((1, tiles_row, TILE), lambda r, s, m: (r, 0, 0)),
            ]
            + [picked(col) for col in range(tiles_row)],
            out_specs=pl.BlockSpec((1, lon_cells, channels), lambda r, s, m: (r, 0, 0)),
        ),
        out_shape=jax.ShapeDtypeStruct(smoothed.shape, jnp.bfloat16),
        compiler_params=pltpu.CompilerParams(vmem_limit_bytes=32 * 1024 * 1024),
        name="merge_tiles",
    )(slot_of, land, smoothed, tile_order, *([results] * tiles_row))


def attend_kernel(x_ref, scale_ref, shift_ref, proj_ref, weight_ref, out_ref):
    parts = x_ref.shape[0]
    width = x_ref.shape[3]
    heads = width // HEAD
    tokens = x_ref.shape[2]
    full = parts * width
    values = [x_ref[g, 0].astype(jnp.float32) for g in range(parts)]
    average = sum(jnp.sum(v, axis=-1, keepdims=True) for v in values) * (1.0 / full)
    centred = [v - average for v in values]
    variance = sum(jnp.sum(v * v, axis=-1, keepdims=True) for v in centred) * (1.0 / full)
    inverse = lax.rsqrt(variance + EPSILON)
    hidden = jnp.concatenate(
        [
            (
                v * inverse * (1.0 + scale_ref[0, :, g * width : (g + 1) * width])
                + shift_ref[0, :, g * width : (g + 1) * width]
            ).astype(jnp.bfloat16)
            for g, v in enumerate(centred)
        ],
        axis=1,
    )
    lane_head = lax.broadcasted_iota(jnp.int32, (TILE, width), 1) // HEAD
    total = jnp.zeros((TILE, full), jnp.float32)
    for g in range(parts):
        queries = jnp.dot(hidden[:TILE], proj_ref[g, 0], preferred_element_type=jnp.float32)
        queries = queries * (1.0 / math.sqrt(HEAD))
        keys = jnp.dot(hidden, proj_ref[g, 1], preferred_element_type=jnp.float32).astype(jnp.bfloat16)
        vals = jnp.dot(hidden, proj_ref[g, 2], preferred_element_type=jnp.float32).astype(jnp.bfloat16)
        stacked = jnp.concatenate(
            [jnp.where(lane_head == h, queries, 0.0).astype(jnp.bfloat16) for h in range(heads)], axis=0
        )
        scores = lax.dot_general(
            stacked, keys, (((1,), (1,)), ((), ())), preferred_element_type=jnp.float32
        )
        weights = jnp.exp(scores - jnp.max(scores, axis=-1, keepdims=True))
        chances = (weights * (1.0 / jnp.sum(weights, axis=-1, keepdims=True))).astype(jnp.bfloat16)
        mixed = jnp.dot(chances, vals, preferred_element_type=jnp.float32)
        mixture = mixed[:TILE]
        for h in range(1, heads):
            mixture = jnp.where(lane_head == h, mixed[h * TILE : (h + 1) * TILE], mixture)
        total = total + jnp.dot(
            mixture.astype(jnp.bfloat16), weight_ref[g], preferred_element_type=jnp.float32
        )
    for g in range(parts):
        out_ref[g, 0] = total[:, g * width : (g + 1) * width].astype(jnp.bfloat16)


def attend(inputs, scale, shift, projection, out_weight):
    parts, slots, tokens, width = inputs.shape
    full = parts * width
    whole = lambda s: (0, 0, 0, 0)
    return pl.pallas_call(
        attend_kernel,
        grid=(slots,),
        in_specs=[
            pl.BlockSpec((parts, 1, tokens, width), lambda s: (0, s, 0, 0)),
            pl.BlockSpec((1, 1, full), lambda s: (s, 0, 0)),
            pl.BlockSpec((1, 1, full), lambda s: (s, 0, 0)),
            pl.BlockSpec(projection.shape, whole),
            pl.BlockSpec(out_weight.shape, lambda s: (0, 0, 0)),
        ],
        out_specs=pl.BlockSpec((parts, 1, TILE, width), lambda s: (0, s, 0, 0)),
        out_shape=jax.ShapeDtypeStruct((parts, slots, TILE, width), jnp.bfloat16),
        compiler_params=pltpu.CompilerParams(vmem_limit_bytes=48 * 1024 * 1024),
        cost_estimate=pl.CostEstimate(
            flops=slots * 2 * tokens * full * full * 4,
            bytes_accessed=2 * (slots * 2 * tokens * full + 4 * full * full),
            transcendentals=slots * tokens * tokens * 8,
        ),
        name="attend",
    )(inputs, scale[:, None, :], shift[:, None, :], projection, out_weight)


def pick_rows(mod_table, first_slot, slot_total, per_source):
    sources = (first_slot + jnp.arange(slot_total, dtype=jnp.int32)) // per_source
    select = (sources[:, None] == jnp.arange(mod_table.shape[0], dtype=jnp.int32)[None, :]).astype(
        jnp.float32
    )
    return jnp.dot(select, mod_table, precision=lax.Precision.HIGHEST)


def body(
    fine_field,
    conv_taps,
    position_table,
    coarse_bands,
    band_weight,
    noise_step,
    land_tiles,
    tile_owner,
    neighbour_lists,
    tile_order,
    expert_projections,
    expert_output,
):
    lat_rows, lon_cells, channels = fine_field.shape
    tiles_row = land_tiles.shape[1]
    tile_count = lat_rows * tiles_row
    strips = lax.axis_size("row")
    per_owner = tile_count // strips
    padded = extended(fine_field, (("row", 0),), 1)
    padded = jnp.pad(padded, ((0, 0), (1, 1), (0, 0)))
    tap_values = conv_taps.astype(jnp.float32)
    running = fine_field.astype(jnp.float32)
    for row_shift in range(3):
        for col_shift in range(3):
            running = running + tap_values[row_shift, col_shift] * padded[
                row_shift : row_shift + lat_rows, col_shift : col_shift + lon_cells
            ].astype(jnp.float32)
    smoothed = running.astype(jnp.bfloat16)
    land_flat = land_tiles.reshape(tile_count)
    owner_flat = tile_owner.reshape(tile_count)
    tile_ids = jnp.arange(tile_count, dtype=jnp.int32)
    earlier = (
        (owner_flat[None, :] == owner_flat[:, None])
        & (land_flat[None, :] > 0)
        & (tile_ids[None, :] < tile_ids[:, None])
    )
    slot_rank = jnp.sum(earlier.astype(jnp.int32), axis=1)
    slot_of = owner_flat * per_owner + slot_rank
    chosen = ((slot_of[None, :] == tile_ids[:, None]) & (land_flat[None, :] > 0)).astype(jnp.int32)
    tile_of = jnp.sum(chosen * tile_ids[None, :], axis=1)
    starts = (tile_ids % tiles_row) * TILE
    index_table = jnp.concatenate(
        [
            tile_order.reshape(tile_count, TILE) + starts[:, None],
            neighbour_lists.reshape(tile_count, TILE),
        ],
        axis=1,
    ).T
    sequence = gather_tiles(smoothed, tile_of, index_table, position_table, tiles_row)
    outgoing = sequence.reshape(strips, per_owner, 2 * TILE, channels)
    group_size = lax.axis_size(("col", "sub"))
    my_slots = tile_count // group_size
    arrived = lax.all_to_all(outgoing, "row", split_axis=0, concat_axis=0, tiled=True)
    arrived = arrived.reshape(group_size, my_slots, 2 * TILE, channels)
    gathered_bands = lax.all_gather(coarse_bands, "row", axis=0, tiled=True)
    band_means = jnp.mean(gathered_bands.astype(jnp.float32), axis=2)
    modulation = jnp.dot(
        band_means, band_weight.astype(jnp.float32), precision=lax.Precision.HIGHEST
    ) + step_embedding(noise_step, band_weight.shape[1])
    full_width = band_weight.shape[1] // 2
    inputs = lax.all_to_all(arrived, ("col", "sub"), split_axis=0, concat_axis=0, tiled=True)
    full_proj = lax.all_gather(
        jnp.transpose(expert_projections[0], (1, 0, 2)), ("col", "sub"), axis=0, tiled=False
    )
    full_out = lax.all_gather(expert_output[0], ("col", "sub"), axis=0, tiled=False)
    local_mod = pick_rows(
        modulation, lax.axis_index(("col", "sub")) * my_slots, my_slots, per_owner
    )
    heads_out = attend(
        inputs, local_mod[:, :full_width], local_mod[:, full_width:], full_proj, full_out
    )
    returned = lax.all_to_all(heads_out, ("col", "sub"), split_axis=0, concat_axis=0, tiled=True)
    returned = returned.reshape(strips, per_owner, TILE, channels)
    results = lax.all_to_all(returned, "row", split_axis=0, concat_axis=0, tiled=True)
    results = results.reshape(tile_count, TILE, channels)
    return merge_tiles(
        smoothed, results, jnp.minimum(slot_of, tile_count - 1), land_flat, tile_order
    )


def solution(mesh):
    placed = (
        P(("grp", "row"), None, ("col", "sub")),
        P(None, None, ("col", "sub")),
        P(None, ("col", "sub")),
        P(("grp", "row"), None, None),
        P(),
        P(),
        P(("grp", "row"), None),
        P(("grp", "row"), None),
        P(("grp", "row"), None, None),
        P(("grp", "row"), None, None),
        P("row", None, None, ("col", "sub")),
        P("row", ("col", "sub"), None),
    )
    return jax.shard_map(
        body,
        mesh=mesh,
        in_specs=placed,
        out_specs=P(("grp", "row"), None, ("col", "sub")),
        check_vma=False,
    )
```

time: 454 us -> 320 us (0.70)
  local copies, waits for them, and re-layouts: 83.2 us -> 5.6 us
  other arithmetic: 64.8 us -> 7.24 us
  waiting for transfers between devices: 91.9 us -> 35.2 us
  Pallas kernels: 0 us -> 54.6 us
  blocking collectives: 139 us -> 190 us
  matrix products: 43.8 us -> 0.41 us
    all_to_all x2 -> x1, waiting for transfers between devices: 89.9 us -> 33.7 us  [body(): lax.all_to_all(arrived, ('col', 'sub'), split_axis=0, concat_axis=0, tile...]
    pallas_call x0 -> x3, Pallas kernels: none -> 54.6 us  [the longest x1 40.1 us: attend(): pl.pallas_call(attend_kernel, grid=(slots,), in_specs=[pl.BlockSpec((part...]
    all_to_all x1 -> x2, blocking collectives: 28.9 us -> 78.7 us  [the longest x1 50.6 us: body(): lax.all_to_all(returned, 'row', split_axis=0, concat_axis=0, tiled=True)]
    gather x3 -> x0, local copies, waits for them, and re-layouts: 35.6 us -> none  [the longest x1 33.1 us: body(): jnp.take(flat_field, cell_index, axis=0).astype(jnp.float32)]
    dot_general x4 -> x0, matrix products: 31.9 us -> none  [the longest x1 12.1 us: attend_block(): jnp.einsum('skd,dtw->sktw', hidden, projection[:, 1:], preferred_element_...]
    scatter-add x1 -> x0, other arithmetic: 29 us -> none  [body(): flat_field.astype(jnp.float32).at[query_cells.reshape(-1)]]
    convert_element_type x3 -> x0, local copies, waits for them, and re-layouts: 26.6 us -> none  [the longest x2 22.7 us: attend_block(): values = inputs.astype(jnp.float32)]
    convert_element_type x7 -> x0, other arithmetic: 23.2 us -> none  [the longest x1 6.46 us: attend_block(): values = inputs.astype(jnp.float32)]
  transfers between devices with their start and end apart: 6 -> 5, of which waited for: 3 -> 2; matrix products, arithmetic and copies ran while one was open for 34% -> 4% of each run, Pallas kernels for 0% -> 3%
where the time goes in v1:
time: 320 us; the launch traced here: 319 us
  blocking collectives  190 us (59%)
  Pallas kernels  54.6 us (17%)
  waiting for transfers between devices  35.2 us (11%)
  between operations  14.3 us (4%)
  starting transfers between devices  11.9 us (4%)
  other arithmetic  7.24 us (2%)
  local copies, waits for them, and re-layouts  5.6 us (2%)
    all_to_all x1, blocking collectives, body(): lax.all_to_all(outgoing, 'row', split_axis=0, concat_axis=0, tiled=True)  97.8 us
    all_to_all x1, blocking collectives, body(): lax.all_to_all(returned, 'row', split_axis=0, concat_axis=0, tiled=True)  50.6 us
    pallas_call x1, Pallas kernels, attend(): pl.pallas_call(attend_kernel, grid=(slots,), in_specs=[pl.BlockSpec((part...  40.1 us
    all_to_all x1, waiting for transfers between devices, body(): lax.all_to_all(arrived, ('col', 'sub'), split_axis=0, concat_axis=0, tile...  33.7 us
    all_to_all x1, blocking collectives, body(): lax.all_to_all(heads_out, ('col', 'sub'), split_axis=0, concat_axis=0, ti...  28.2 us
    all_gather x1, blocking collectives, body(): gathered_bands = lax.all_gather(coarse_bands, 'row', axis=0, tiled=True)  13.1 us
    pallas_call x1, Pallas kernels, gather_tiles(): pl.pallas_call(gather_kernel, grid_spec=pltpu.PrefetchScalarGridSpec(num_...  10 us
  transfers between devices with their start and end apart: 5, of which 2 were waited for; matrix products, arithmetic and copies ran while one was open for 4% of the time, Pallas kernels for 3%

profile of v1, /device:TPU:0, one launch (start us, length us, event | category | flops | bytes accessed | tf_op | source)
XLA Modules:
  0.0 318.9 jit_solution(14219383173383348718)
XLA Ops:
  6.5 0.7 all-gather.4.cloned.1.call-update
  7.3 1.1 fusion.23
  8.4 1.3 collective-permute-start.1
  9.7 5.6 %collective-permute-start = (bf16[1,512,256]{2,1,0:T(8,128)(2,1)S(1)}, bf16[1,512,256]{2,1,0:T(8,128)(2,1)S(1)}, u32[]{:S(2)}, u32[]{:S(2)}) collective-permute-start(bf16[1,512,256]{2,1,0:T(8,128)(2,1)S(1)} %get-tuple-element.7), channel_id=1, source_target_pairs={{0,4},{4,8},{8,12},{1,5},{5,9},{9,13},{2,6},{6,10},{10,14},{3,7},{... | collective-permute-start | bytes 786440 | tf_op jit(solution)/shard_map/ppermute | solution.py:26
  15.3 0.8 copy.24
  16.1 0.8 copy.25
  17.2 0.8 broadcast_add_fusion
  18.0 0.7 pad_add_fusion
  18.9 1.1 fusion.25
  20.0 0.8 collective-permute-done
  20.8 0.9 fusion.14
  21.7 4.3 %fusion.9.field_ref = bf16[8,512,256]{2,1,0:T(8,128)(2,1)S(1)} fusion(bf16[8,512,256]{2,1,0:T(8,128)(2,1)S(1)} %copy-done.5, bf16[10,514,256]{2,1,0:T(8,128)(2,1)S(1)} %fusion.14, bf16[1,512,256]{2,1,0:T(8,128)(2,1)S(1)} %collective-permute-done.1, bf16[1,512,256]{2,1,0:T(8,128)(2,1)S(1)} %collective-permute-done, f32[256]{0:T(256)S(1)} %bitcast.38, ...), kind=kLoop, calls=%fused_computation.13 | loop fusion | flops 31457280 | bytes 17310720 | tf_op jit(solution)/shard_map/convert_element_type | solution.py:229
  26.1 10.0 %gather_tiles.1 = bf16[32,256,256]{2,1,0:T(8,128)(2,1)S(1)} custom-call(s32[32]{0:T(128)S(1)} %select_reduce_fusion.tile_ref, bf16[8,512,256]{2,1,0:T(8,128)(2,1)S(1)} %fusion.9.field_ref, s32[256,32]{1,0:T(8,128)S(1)} %bitcast.26, bf16[256,256]{1,0:T(8,128)(2,1)S(1)} %copy-done.3), custom_call_target="tpu_custom_call" | custom-call | flops 2147483648 | bytes 12582912 | tf_op jit(solution)/shard_map/gather_tiles/pallas_call | solution.py:56
  36.1 97.8 %all_to_all.20 = bf16[4,8,256,256]{3,2,1,0:T(8,128)(2,1)} all-to-all(bf16[4,8,256,256]{3,2,1,0:T(8,128)(2,1)S(1)} %bitcast.25), channel_id=1, replica_groups=mesh['grp'=2,'row'=4,'col'=2,'sub'=2] {'row'}, dimensions={0} | all-to-all | bytes 8388608 | tf_op jit(solution)/shard_map/all_to_all | solution.py:254
  133.9 5.0 %all-to-all-start.1 = ((bf16[4,8,256,256]{3,2,1,0:T(8,128)(2,1)}), bf16[4,8,256,256]{3,2,1,0:T(8,128)(2,1)}, u32[]{:S(2)}, u32[]{:S(2)}) async-start(bf16[4,8,256,256]{3,2,1,0:T(8,128)(2,1)} %all_to_all.20), calls=%async_computation.1 | async-start | bytes 8388608 | tf_op jit(solution)/shard_map/all_to_all | solution.py:262
  139.5 13.1 %all_gather.12 = bf16[4,34,64]{2,1,0:T(8,128)(2,1)S(1)} all-gather(bf16[1,34,64]{2,1,0:T(8,128)(2,1)S(1)} %copy-done.6), channel_id=1, replica_groups=mesh['grp'=2,'row'=4,'col'=2,'sub'=2] {'row'}, dimensions={0}, use_global_device_ids=true | all-gather | bytes 21760 | tf_op jit(solution)/shard_map/all_gather | solution.py:256
  152.9 0.2 convolution_add_fusion
  153.1 0.2 fusion.17
  153.4 33.7 %all-to-all-done.1.x_ref = bf16[4,8,256,256]{3,2,1,0:T(8,128)(2,1)} async-done(((bf16[4,8,256,256]{3,2,1,0:T(8,128)(2,1)}), bf16[4,8,256,256]{3,2,1,0:T(8,128)(2,1)}, u32[]{:S(2)}, u32[]{:S(2)}) %all-to-all-start.1) | async-done | bytes 4194336 | tf_op jit(solution)/shard_map/all_to_all | solution.py:262
  187.1 1.6 copy-done.2
  188.7 40.1 %attend.1 = bf16[4,8,128,256]{3,2,1,0:T(8,128)(2,1)S(1)} custom-call(bf16[4,8,256,256]{3,2,1,0:T(8,128)(2,1)} %all-to-all-done.1.x_ref, f32[8,1,1024]{2,1,0:T(1,128)S(1)} %broadcast_in_dim.4.scale_ref, f32[8,1,1024]{2,1,0:T(1,128)S(1)} %broadcast_in_dim.5.shift_ref, bf16[4,3,1024,256]{3,2,1,0:T(8,128)(2,1)} %bitcast.39, bf16[4,256,1024]{2,1,0:T(8,128)(2,1)S(1)} %copy-done.2), custom_call_target="tpu_custom_call" | custom-call | flops 17179869184 | bytes 16777216 | tf_op jit(solution)/shard_map/attend/pallas_call | solution.py:171
  228.8 28.2 %all_to_all.21 = bf16[4,8,128,256]{3,2,1,0:T(8,128)(2,1)S(1)} all-to-all(bf16[4,8,128,256]{3,2,1,0:T(8,128)(2,1)S(1)} %attend.1), channel_id=1, replica_groups=mesh['grp'=2,'row'=4,'col'=2,'sub'=2] {'col','sub'}, dimensions={0} | all-to-all | bytes 4194304 | tf_op jit(solution)/shard_map/all_to_all | solution.py:273
  256.9 50.6 %all_to_all.22 = bf16[4,8,128,256]{3,2,1,0:T(8,128)(2,1)S(1)} all-to-all(bf16[4,8,128,256]{3,2,1,0:T(8,128)(2,1)S(1)} %all_to_all.21), channel_id=1, replica_groups=mesh['grp'=2,'row'=4,'col'=2,'sub'=2] {'row'}, dimensions={0} | all-to-all | bytes 4194304 | tf_op jit(solution)/shard_map/all_to_all | solution.py:275
  307.5 4.5 %merge_tiles.1 = bf16[8,512,256]{2,1,0:T(8,128)(2,1)} custom-call(s32[32]{0:T(128)S(1)} %get-tuple-element.5.slot_ref, s32[32]{0:T(128)S(1)} %broadcast_in_dim_reshape.2.land_ref, bf16[8,512,256]{2,1,0:T(8,128)(2,1)S(1)} %fusion.9.field_ref, s32[8,4,128]{2,1,0:T(4,128)S(1)} %copy-done.1, bf16[32,128,256]{2,1,0:T(8,128)(2,1)S(1)} %bitcast.21, ...), custom_call_target="tpu_custom_call" | custom-call | tf_op jit(solution)/shard_map/merge_tiles/pallas_call | solution.py:102
  (33 shorter events, 0.9 us)
Async XLA Ops:
  6.5 146.3 %copy-start = (bf16[34,2048]{1,0:T(8,128)(2,1)S(1)}, bf16[34,2048]{1,0:T(8,128)(2,1)}, u32[]{:S(2)}) copy-start(bf16[34,2048]{1,0:T(8,128)(2,1)} %param.16) | copy-start | bytes 417796
  6.5 14.3 %copy-start.4 = (bf16[8,512,256]{2,1,0:T(8,128)(2,1)S(1)}, bf16[8,512,256]{2,1,0:T(8,128)(2,1)}, u32[]{:S(2)}) copy-start(bf16[8,512,256]{2,1,0:T(8,128)(2,1)} %param.12) | copy-start | bytes 6291460
  6.5 146.9 %all-gather.4.cloned.1.call-start = ((), (), s32[]{:S(2)}) async-start(), calls=%async_computation.4 | async-start | bytes 2621440 | tf_op jit(solution)/shard_map/all_gather | solution.py:266
  7.3 146.2 %all-gather.6.cloned.1.call-start = ((), (), s32[]{:S(2)}) async-start(), calls=%async_computation.5 | async-start | bytes 7864320 | tf_op jit(solution)/shard_map/all_gather | solution.py:263
  8.4 11.6 %collective-permute-start.1 = (bf16[1,512,256]{2,1,0:T(8,128)(2,1)S(1)}, bf16[1,512,256]{2,1,0:T(8,128)(2,1)S(1)}, u32[]{:S(2)}, u32[]{:S(2)}) collective-permute-start(bf16[1,512,256]{2,1,0:T(8,128)(2,1)S(1)} %get-tuple-element.8), channel_id=1, source_target_pairs={{4,0},{8,4},{12,8},{5,1},{9,5},{13,9},{6,2},{10,6},{14,10},{7,3},{... | collective-permute-start | bytes 786440 | tf_op jit(solution)/shard_map/ppermute | solution.py:28
  9.7 11.1 %collective-permute-start = (bf16[1,512,256]{2,1,0:T(8,128)(2,1)S(1)}, bf16[1,512,256]{2,1,0:T(8,128)(2,1)S(1)}, u32[]{:S(2)}, u32[]{:S(2)}) collective-permute-start(bf16[1,512,256]{2,1,0:T(8,128)(2,1)S(1)} %get-tuple-element.7), channel_id=1, source_target_pairs={{0,4},{4,8},{8,12},{1,5},{5,9},{9,13},{2,6},{6,10},{10,14},{3,7},{... | collective-permute-start | bytes 786440 | tf_op jit(solution)/shard_map/ppermute | solution.py:26
  18.9 2.8 copy-start.5
  21.7 4.4 %copy-start.3 = (bf16[256,256]{1,0:T(8,128)(2,1)S(1)}, bf16[256,256]{1,0:T(8,128)(2,1)}, u32[]{:S(2)}) copy-start(bf16[256,256]{1,0:T(8,128)(2,1)} %table_ref.1) | copy-start | bytes 393220
  133.9 5.6 %copy-start.6 = (bf16[1,34,64]{2,1,0:T(8,128)(2,1)S(1)}, bf16[1,34,64]{2,1,0:T(8,128)(2,1)}, u32[]{:S(2)}) copy-start(bf16[1,34,64]{2,1,0:T(8,128)(2,1)} %param.15) | copy-start | bytes 13060
  133.9 53.2 %all-to-all-start.1 = ((bf16[4,8,256,256]{3,2,1,0:T(8,128)(2,1)}), bf16[4,8,256,256]{3,2,1,0:T(8,128)(2,1)}, u32[]{:S(2)}, u32[]{:S(2)}) async-start(bf16[4,8,256,256]{3,2,1,0:T(8,128)(2,1)} %all_to_all.20), calls=%async_computation.1 | async-start | bytes 8388608 | tf_op jit(solution)/shard_map/all_to_all | solution.py:262
  187.1 1.6 copy-start.2
  228.8 78.7 %copy-start.1 = (s32[8,4,128]{2,1,0:T(4,128)S(1)}, s32[8,4,128]{2,1,0:T(4,128)}, u32[]{:S(2)}) copy-start(s32[8,4,128]{2,1,0:T(4,128)} %order_ref.1) | copy-start | bytes 49156
Sparse Core Ops, SparseCore 0:
  8.9 25.2 all-gather.3
  35.8 46.3 all-gather.5

commit v2 on v1

--- a/solution.py
+++ b/solution.py
@@ -188,6 +188,92 @@
         ),
         name="attend",
     )(inputs, scale[:, None, :], shift[:, None, :], projection, out_weight)
+
+
+def exchange_kernel(strips, group, forward, src_ref, dst_ref, send_sems, recv_sems, local_sem):
+    row = lax.axis_index("row")
+    subs = lax.axis_size("sub")
+    mine = lax.axis_index("col") * subs + lax.axis_index("sub")
+    share = (dst_ref if forward else src_ref).shape[1] // strips
+
+    def target(step):
+        there = lax.rem(row + step // group, strips)
+        member = lax.rem(mine + step % group, group)
+        return there, member
+
+    def ends(there, member):
+        if forward:
+            source = src_ref.at[there, pl.ds(member * share, share)]
+            return source, dst_ref.at[mine, pl.ds(row * share, share)]
+        source = src_ref.at[member, pl.ds(there * share, share)]
+        return source, dst_ref.at[row, pl.ds(mine * share, share)]
+
+    def device(there, member):
+        return {"row": there, "col": member // subs, "sub": lax.rem(member, subs)}
+
+    def remote(step):
+        there, member = target(step)
+        source, dest = ends(there, member)
+        return pltpu.make_async_remote_copy(
+            src_ref=source,
+            dst_ref=dest,
+            send_sem=send_sems.at[step],
+            recv_sem=recv_sems.at[step],
+            device_id=device(there, member),
+            device_id_type=pl.DeviceIdType.MESH,
+        )
+
+    total = strips * group
+    barrier = pltpu.get_barrier_semaphore()
+    source, dest = ends(row, mine)
+    local = pltpu.make_async_copy(source, dest, local_sem)
+    local.start()
+
+    @pl.loop(1, total)
+    def _(step):
+        there, member = target(step)
+        pl.semaphore_signal(
+            barrier, inc=1, device_id=device(there, member), device_id_type=pl.DeviceIdType.MESH
+        )
+
+    pl.semaphore_wait(barrier, total - 1)
+
+    @pl.loop(1, total)
+    def _(step):
+        remote(total - step).start()
+
+    local.wait()
+
+    @pl.loop(1, total)
+    def _(step):
+        remote(step).wait()
+
+
+def exchange(array, strips, group, forward):
+    first, second, tokens, width = array.shape
+    if forward:
+        shape = (group, strips * (second // group), tokens, width)
+    else:
+        shape = (strips, group * (second // strips), tokens, width)
+    total = strips * group
+    return pl.pallas_call(
+        functools.partial(exchange_kernel, strips, group, forward),
+        out_shape=jax.ShapeDtypeStruct(shape, array.dtype),
+        in_specs=[pl.BlockSpec(memory_space=pl.ANY)],
+        out_specs=pl.BlockSpec(memory_space=pl.ANY),
+        scratch_shapes=[
+            pltpu.SemaphoreType.DMA((total,)),
+            pltpu.SemaphoreType.DMA((total,)),
+            pltpu.SemaphoreType.DMA,
+        ],
+        compiler_params=pltpu.CompilerParams(
+            collective_id=0 if forward else 1, has_side_effects=True
+        ),
+        cost_estimate=pl.CostEstimate(
+            flops=0, bytes_accessed=(64 if forward else 32) * array.size, transcendentals=0
+        ),
+        name="send_tiles" if forward else "return_tiles",
+    )(array)
 
 
 def pick_rows(mod_table, first_slot, slot_total, per_source):
@@ -251,28 +337,38 @@
     outgoing = sequence.reshape(strips, per_owner, 2 * TILE, channels)
     group_size = lax.axis_size(("col", "sub"))
     my_slots = tile_count // group_size
-    arrived = lax.all_to_all(outgoing, "row", split_axis=0, concat_axis=0, tiled=True)
-    arrived = arrived.reshape(group_size, my_slots, 2 * TILE, channels)
+    direct = per_owner % group_size == 0
     gathered_bands = lax.all_gather(coarse_bands, "row", axis=0, tiled=True)
     band_means = jnp.mean(gathered_bands.astype(jnp.float32), axis=2)
     modulation = jnp.dot(
         band_means, band_weight.astype(jnp.float32), precision=lax.Precision.HIGHEST
     ) + step_embedding(noise_step, band_weight.shape[1])
     full_width = band_weight.shape[1] // 2
-    inputs = lax.all_to_all(arrived, ("col", "sub"), split_axis=0, concat_axis=0, tiled=True)
+    if direct:
+        inputs = exchange(outgoing, strips, group_size, True)
+    else:
+        arrived = lax.all_to_all(outgoing, "row", split_axis=0, concat_axis=0, tiled=True)
+        arrived = arrived.reshape(group_size, my_slots, 2 * TILE, channels)
+        inputs = lax.all_to_all(arrived, ("col", "sub"), split_axis=0, concat_axis=0, tiled=True)
     full_proj = lax.all_gather(
         jnp.transpose(expert_projections[0], (1, 0, 2)), ("col", "sub"), axis=0, tiled=False
     )
     full_out = lax.all_gather(expert_output[0], ("col", "sub"), axis=0, tiled=False)
-    local_mod = pick_rows(
-        modulation, lax.axis_index(("col", "sub")) * my_slots, my_slots, per_owner
-    )
+    if direct:
+        local_mod = pick_rows(modulation, 0, my_slots, per_owner // group_size)
+    else:
+        local_mod = pick_rows(
+            modulation, lax.axis_index(("col", "sub")) * my_slots, my_slots, per_owner
+        )
     heads_out = attend(
         inputs, local_mod[:, :full_width], local_mod[:, full_width:], full_proj, full_out
     )
-    returned = lax.all_to_all(heads_out, ("col", "sub"), split_axis=0, concat_axis=0, tiled=True)
-    returned = returned.reshape(strips, per_owner, TILE, channels)
-    results = lax.all_to_all(returned, "row", split_axis=0, concat_axis=0, tiled=True)
+    if direct:
+        results = exchange(heads_out, strips, group_size, False)
+    else:
+        returned = lax.all_to_all(heads_out, ("col", "sub"), split_axis=0, concat_axis=0, tiled=True)
+        returned = returned.reshape(strips, per_owner, TILE, channels)
+        results = lax.all_to_all(returned, "row", split_axis=0, concat_axis=0, tiled=True)
     results = results.reshape(tile_count, TILE, channels)
     return merge_tiles(
         smoothed, results, jnp.minimum(slot_of, tile_count - 1), land_flat, tile_order

time: 320 us -> 255 us (0.80)
  blocking collectives: 190 us -> 14 us
  Pallas kernels: 54.6 us -> 199 us
  waiting for transfers between devices: 35.2 us -> 1.45 us
  starting transfers between devices: 11.9 us -> 6.9 us
  local copies, waits for them, and re-layouts: 5.6 us -> 10.4 us
    all_to_all x3 -> x0, blocking collectives: 177 us -> none  [the longest x1 97.8 us: body(): lax.all_to_all(outgoing, 'row', split_axis=0, concat_axis=0, tiled=True)]
    pallas_call x0 -> x2, Pallas kernels: none -> 145 us  [exchange(): pl.pallas_call(functools.partial(exchange_kernel, strips, group, forward)...]
    all_to_all x1 -> x0, waiting for transfers between devices: 33.7 us -> none  [body(): lax.all_to_all(arrived, ('col', 'sub'), split_axis=0, concat_axis=0, tile...]
    all_to_all x1 -> x0, starting transfers between devices: 4.98 us -> none  [body(): lax.all_to_all(arrived, ('col', 'sub'), split_axis=0, concat_axis=0, tile...]
    unnamed x16 -> x20, local copies, waits for them, and re-layouts: 3.14 us -> 8.07 us
  transfers between devices with their start and end apart: 5 -> 4, of which waited for: 2 -> 0; matrix products, arithmetic and copies ran while one was open for 4% -> 5% of each run, Pallas kernels for 3% -> 41%
where the time goes in v2:
time: 255 us; the launch traced here: 254 us
  Pallas kernels  199 us (78%)
  between operations  14.3 us (6%)
  blocking collectives  14 us (5%)
  local copies, waits for them, and re-layouts  10.4 us (4%)
  other arithmetic  7.24 us (3%)
  starting transfers between devices  6.9 us (3%)
    pallas_call x2, Pallas kernels, exchange(): pl.pallas_call(functools.partial(exchange_kernel, strips, group, forward)...  145 us
    pallas_call x1, Pallas kernels, attend(): pl.pallas_call(attend_kernel, grid=(slots,), in_specs=[pl.BlockSpec((part...  40 us
    all_gather x1, blocking collectives, body(): gathered_bands = lax.all_gather(coarse_bands, 'row', axis=0, tiled=True)  14 us
    pallas_call x1, Pallas kernels, gather_tiles(): pl.pallas_call(gather_kernel, grid_spec=pltpu.PrefetchScalarGridSpec(num_...  10 us
    unnamed x20, local copies, waits for them, and re-layouts  8.07 us
    ppermute x1, starting transfers between devices, extended(): lax.ppermute(tail, axis, [(i, (i + 1) % count) for i in range(ends)])  5.57 us
  transfers between devices with their start and end apart: 4, of which 0 were waited for; matrix products, arithmetic and copies ran while one was open for 5% of the time, Pallas kernels for 41%

profile of v2, /device:TPU:0, one launch (start us, length us, event | category | flops | bytes accessed | tf_op | source)
XLA Modules:
  0.0 254.2 jit_solution(14824620949415081322)
XLA Ops:
  6.5 0.7 all-gather.4.cloned.1.call-update
  7.3 0.7 all-gather.6.cloned.1.call-update
  8.0 1.1 fusion.23
  9.1 1.3 collective-permute-start.1
  10.4 5.6 %collective-permute-start = (bf16[1,512,256]{2,1,0:T(8,128)(2,1)S(1)}, bf16[1,512,256]{2,1,0:T(8,128)(2,1)S(1)}, u32[]{:S(2)}, u32[]{:S(2)}) collective-permute-start(bf16[1,512,256]{2,1,0:T(8,128)(2,1)S(1)} %get-tuple-element.7), channel_id=1, source_target_pairs={{0,4},{4,8},{8,12},{1,5},{5,9},{9,13},{2,6},{6,10},{10,14},{3,7},{... | collective-permute-start | bytes 786440 | tf_op jit(solution)/shard_map/ppermute | solution.py:26
  16.0 0.8 copy.24
  16.8 0.8 copy.25
  18.3 14.0 %all_gather.12 = bf16[4,34,64]{2,1,0:T(8,128)(2,1)S(1)} all-gather(bf16[1,34,64]{2,1,0:T(8,128)(2,1)} %param.15), channel_id=1, replica_groups=mesh['grp'=2,'row'=4,'col'=2,'sub'=2] {'row'}, dimensions={0}, use_global_device_ids=true | all-gather | bytes 21760 | tf_op jit(solution)/shard_map/all_gather | solution.py:341
  32.4 0.8 broadcast_add_fusion
  33.2 0.7 pad_add_fusion
  34.2 0.2 convolution_add_fusion
  34.4 0.2 fusion.17
  35.0 0.9 fusion.25
  35.9 0.9 fusion.14
  36.9 4.3 %fusion.9.field_ref = bf16[8,512,256]{2,1,0:T(8,128)(2,1)S(1)} fusion(bf16[8,512,256]{2,1,0:T(8,128)(2,1)S(1)} %copy-done.8, bf16[10,514,256]{2,1,0:T(8,128)(2,1)S(1)} %fusion.14, bf16[1,512,256]{2,1,0:T(8,128)(2,1)S(1)} %collective-permute-done.1, bf16[1,512,256]{2,1,0:T(8,128)(2,1)S(1)} %collective-permute-done, f32[256]{0:T(256)S(1)} %bitcast.38, ...), kind=kLoop, calls=%fused_computation.13 | loop fusion | flops 31457280 | bytes 17310720 | tf_op jit(solution)/shard_map/convert_element_type | solution.py:315
  41.2 10.0 %gather_tiles.1 = bf16[32,256,256]{2,1,0:T(8,128)(2,1)S(1)} custom-call(s32[32]{0:T(128)S(1)} %select_reduce_fusion.tile_ref, bf16[8,512,256]{2,1,0:T(8,128)(2,1)S(1)} %fusion.9.field_ref, s32[256,32]{1,0:T(8,128)S(1)} %bitcast.26, bf16[256,256]{1,0:T(8,128)(2,1)S(1)} %copy-done.6), custom_call_target="tpu_custom_call" | custom-call | flops 2147483648 | bytes 12582912 | tf_op jit(solution)/shard_map/gather_tiles/pallas_call | solution.py:56
  51.3 2.0 copy-done.2
  53.4 95.3 %send_tiles.1.x_ref = bf16[4,8,256,256]{3,2,1,0:T(8,128)(2,1)} custom-call(bf16[4,8,256,256]{3,2,1,0:T(8,128)(2,1)} %bitcast.25), custom_call_target="tpu_custom_call" | custom-call | bytes 134217728 | tf_op jit(solution)/shard_map/send_tiles/pallas_call | solution.py:259
  148.7 1.6 copy-done.5
  150.3 40.0 %attend.1.src_ref = bf16[4,8,128,256]{3,2,1,0:T(8,128)(2,1)S(1)} custom-call(bf16[4,8,256,256]{3,2,1,0:T(8,128)(2,1)} %send_tiles.1.x_ref, f32[8,1,1024]{2,1,0:T(1,128)S(1)} %broadcast_in_dim.4.scale_ref, f32[8,1,1024]{2,1,0:T(1,128)S(1)} %broadcast_in_dim.5.shift_ref, bf16[4,3,1024,256]{3,2,1,0:T(8,128)(2,1)} %bitcast.39, bf16[4,256,1024]{2,1,0:T(8,128)(2,1)S(1)} %copy-done.5), custom_call_target="tpu_custom_call" | custom-call | flops 17179869184 | bytes 16777216 | tf_op jit(solution)/shard_map/attend/pallas_call | solution.py:171
  190.4 1.3 copy-done.3
  191.7 49.5 %return_tiles.1 = bf16[4,8,128,256]{3,2,1,0:T(8,128)(2,1)} custom-call(bf16[4,8,128,256]{3,2,1,0:T(8,128)(2,1)} %copy-done.3), custom_call_target="tpu_custom_call" | custom-call | bytes 33554432 | tf_op jit(solution)/shard_map/return_tiles/pallas_call | solution.py:259
  241.3 1.6 copy-done.1
  242.8 4.5 %merge_tiles.1 = bf16[8,512,256]{2,1,0:T(8,128)(2,1)} custom-call(s32[32]{0:T(128)S(1)} %get-tuple-element.5.slot_ref, s32[32]{0:T(128)S(1)} %broadcast_in_dim_reshape.2.land_ref, bf16[8,512,256]{2,1,0:T(8,128)(2,1)S(1)} %fusion.9.field_ref, s32[8,4,128]{2,1,0:T(4,128)S(1)} %copy-done.4, bf16[32,128,256]{2,1,0:T(8,128)(2,1)S(1)} %bitcast.21, ...), custom_call_target="tpu_custom_call" | custom-call | tf_op jit(solution)/shard_map/merge_tiles/pallas_call | solution.py:102
  (34 shorter events, 0.9 us)
Async XLA Ops:
  6.5 27.7 %copy-start = (bf16[34,2048]{1,0:T(8,128)(2,1)S(1)}, bf16[34,2048]{1,0:T(8,128)(2,1)}, u32[]{:S(2)}) copy-start(bf16[34,2048]{1,0:T(8,128)(2,1)} %param.16) | copy-start | bytes 417796
  6.5 29.4 %copy-start.7 = (bf16[8,512,256]{2,1,0:T(8,128)(2,1)S(1)}, bf16[8,512,256]{2,1,0:T(8,128)(2,1)}, u32[]{:S(2)}) copy-start(bf16[8,512,256]{2,1,0:T(8,128)(2,1)} %param.12) | copy-start | bytes 6291460
  6.5 142.1 %all-gather.4.cloned.1.call-start = ((), (), s32[]{:S(2)}) async-start(), calls=%async_computation | async-start | bytes 2621440 | tf_op jit(solution)/shard_map/all_gather | solution.py:356
  7.3 141.4 %all-gather.6.cloned.1.call-start = ((), (), s32[]{:S(2)}) async-start(), calls=%async_computation.1 | async-start | bytes 7864320 | tf_op jit(solution)/shard_map/all_gather | solution.py:353
  9.1 26.8 %collective-permute-start.1 = (bf16[1,512,256]{2,1,0:T(8,128)(2,1)S(1)}, bf16[1,512,256]{2,1,0:T(8,128)(2,1)S(1)}, u32[]{:S(2)}, u32[]{:S(2)}) collective-permute-start(bf16[1,512,256]{2,1,0:T(8,128)(2,1)S(1)} %get-tuple-element.8), channel_id=1, source_target_pairs={{4,0},{8,4},{12,8},{5,1},{9,5},{13,9},{6,2},{10,6},{14,10},{7,3},{... | collective-permute-start | bytes 786440 | tf_op jit(solution)/shard_map/ppermute | solution.py:28
  10.4 25.5 %collective-permute-start = (bf16[1,512,256]{2,1,0:T(8,128)(2,1)S(1)}, bf16[1,512,256]{2,1,0:T(8,128)(2,1)S(1)}, u32[]{:S(2)}, u32[]{:S(2)}) collective-permute-start(bf16[1,512,256]{2,1,0:T(8,128)(2,1)S(1)} %get-tuple-element.7), channel_id=1, source_target_pairs={{0,4},{4,8},{8,12},{1,5},{5,9},{9,13},{2,6},{6,10},{10,14},{3,7},{... | collective-permute-start | bytes 786440 | tf_op jit(solution)/shard_map/ppermute | solution.py:26
  34.9 2.0 copy-start.8
  36.9 4.4 %copy-start.6 = (bf16[256,256]{1,0:T(8,128)(2,1)S(1)}, bf16[256,256]{1,0:T(8,128)(2,1)}, u32[]{:S(2)}) copy-start(bf16[256,256]{1,0:T(8,128)(2,1)} %table_ref.1) | copy-start | bytes 393220
  51.3 2.0 copy-start.2
  148.7 1.6 copy-start.5
  190.4 1.3 copy-start.3
  191.7 49.6 %copy-start.4 = (s32[8,4,128]{2,1,0:T(4,128)S(1)}, s32[8,4,128]{2,1,0:T(4,128)}, u32[]{:S(2)}) copy-start(s32[8,4,128]{2,1,0:T(4,128)} %order_ref.1) | copy-start | bytes 49156
  241.2 1.6 copy-start.1
Sparse Core Ops, SparseCore 0:
  8.9 25.3 all-gather.3
  35.8 69.0 all-gather.5

commit v3 on v1

--- a/solution.py
+++ b/solution.py
@@ -117,13 +117,10 @@
     )(slot_of, land, smoothed, tile_order, *([results] * tiles_row))
 
 
-def attend_kernel(x_ref, scale_ref, shift_ref, proj_ref, weight_ref, out_ref):
-    parts = x_ref.shape[0]
-    width = x_ref.shape[3]
+def attend_slot(values, scale, shift, proj_ref, weight_ref):
+    parts, width = len(values), values[0].shape[1]
     heads = width // HEAD
-    tokens = x_ref.shape[2]
     full = parts * width
-    values = [x_ref[g, 0].astype(jnp.float32) for g in range(parts)]
     average = sum(jnp.sum(v, axis=-1, keepdims=True) for v in values) * (1.0 / full)
     centred = [v - average for v in values]
     variance = sum(jnp.sum(v * v, axis=-1, keepdims=True) for v in centred) * (1.0 / full)
@@ -131,8 +128,8 @@
     hidden = jnp.concatenate(
         [
             (
-                v * inverse * (1.0 + scale_ref[0, :, g * width : (g + 1) * width])
-                + shift_ref[0, :, g * width : (g + 1) * width]
+                v * inverse * (1.0 + scale[:, g * width : (g + 1) * width])
+                + shift[:, g * width : (g + 1) * width]
             ).astype(jnp.bfloat16)
             for g, v in enumerate(centred)
         ],
@@ -160,8 +157,244 @@
         total = total + jnp.dot(
             mixture.astype(jnp.bfloat16), weight_ref[g], preferred_element_type=jnp.float32
         )
-    for g in range(parts):
-        out_ref[g, 0] = total[:, g * width : (g + 1) * width].astype(jnp.bfloat16)
+    return [total[:, g * width : (g + 1) * width].astype(jnp.bfloat16) for g in range(parts)]
+
+
+def attend_kernel(x_ref, scale_ref, shift_ref, proj_ref, weight_ref, out_ref):
+    values = [x_ref[g, 0].astype(jnp.float32) for g in range(x_ref.shape[0])]
+    pieces = attend_slot(values, scale_ref[0], shift_ref[0], proj_ref, weight_ref)
+    for g, piece in enumerate(pieces):
+        out_ref[g, 0] = piece
+
+
+def travel_kernel(
+    strips,
+    cols,
+    subs,
+    seq_ref,
+    mod_ref,
+    own_proj_ref,
+    own_weight_ref,
+    out_ref,
+    tokens,
+    mods,
+    proj,
+    weight,
+    done,
+    seq_send,
+    seq_recv,
+    back_send,
+    back_recv,
+    mod_send,
+    mod_recv,
+    far_send,
+    far_recv,
+    near_send,
+    near_recv,
+    local_sems,
+):
+    group = cols * subs
+    total = strips * group
+    row = lax.axis_index("row")
+    col = lax.axis_index("col")
+    sub = lax.axis_index("sub")
+    mine = col * subs + sub
+    slots = tokens.shape[1]
+    share = slots // strips
+    full = mods.shape[2] // 2
+
+    def device(there, member):
+        return {"row": there, "col": member // subs, "sub": lax.rem(member, subs)}
+
+    def remote(source, dest, send, recv, there, member):
+        return pltpu.make_async_remote_copy(
+            src_ref=source,
+            dst_ref=dest,
+            send_sem=send,
+            recv_sem=recv,
+            device_id=device(there, member),
+            device_id_type=pl.DeviceIdType.MESH,
+        )
+
+    def seq_ends(there, member):
+        return (
+            seq_ref.at[there, pl.ds(member * share, share)],
+            tokens.at[mine, pl.ds(row * share, share)],
+        )
+
+    def seq_copy(step):
+        there, member = lax.rem(row + step // group, strips), lax.rem(mine + step % group, group)
+        source, dest = seq_ends(there, member)
+        return remote(source, dest, seq_send.at[step], seq_recv.at[step], there, member)
+
+    def back_ends(there, member):
+        return (
+            done.at[member, pl.ds(there * share, share)],
+            out_ref.at[row, pl.ds(mine * share, share)],
+        )
+
+    def back_copy(step):
+        there = lax.rem(row + strips - step // group, strips)
+        member = lax.rem(mine + step % group, group)
+        source, dest = back_ends(there, member)
+        return remote(source, dest, back_send.at[step], back_recv.at[step], there, member)
+
+    def mod_copy(step):
+        there = lax.rem(row + step, strips)
+        return remote(mod_ref, mods.at[row], mod_send.at[step], mod_recv.at[step], there, mine)
+
+    pairs = ((own_proj_ref, proj), (own_weight_ref, weight))
+
+    def far_copy(step, kind):
+        source, held = pairs[kind]
+        member = lax.rem(col + step, cols) * subs + sub
+        at = step * 2 + kind
+        return remote(source, held.at[mine], far_send.at[at], far_recv.at[at], row, member)
+
+    def near_copy(step, hop, kind):
+        source, held = pairs[kind]
+        owner = lax.rem(col + cols - step, cols) * subs + sub
+        member = col * subs + lax.rem(sub + hop, subs)
+        at = (step * subs + hop) * 2 + kind
+        return remote(
+            source if step == 0 else held.at[owner],
+            held.at[owner],
+            near_send.at[at],
+            near_recv.at[at],
+            row,
+            member,
+        )
+
+    seq_local = pltpu.make_async_copy(*seq_ends(row, mine), local_sems.at[0])
+    back_local = pltpu.make_async_copy(*back_ends(row, mine), local_sems.at[1])
+    locals_ = [
+        pltpu.make_async_copy(mod_ref, mods.at[row], local_sems.at[2]),
+        pltpu.make_async_copy(own_proj_ref, proj.at[mine], local_sems.at[3]),
+        pltpu.make_async_copy(own_weight_ref, weight.at[mine], local_sems.at[4]),
+    ]
+    seq_local.start()
+    for copy in locals_:
+        copy.start()
+
+    barrier = pltpu.get_barrier_semaphore()
+
+    @pl.loop(1, total)
+    def _(step):
+        there, member = lax.rem(row + step // group, strips), lax.rem(mine + step % group, group)
+        pl.semaphore_signal(
+            barrier, inc=1, device_id=device(there, member), device_id_type=pl.DeviceIdType.MESH
+        )
+
+    pl.semaphore_wait(barrier, total - 1)
+
+    for kind in range(2):
+        for step in range(1, cols):
+            far_copy(step, kind).start()
+        for hop in range(1, subs):
+            near_copy(0, hop, kind).start()
+    for step in range(1, strips):
+        mod_copy(step).start()
+
+    @pl.loop(1, total)
+    def _(step):
+        seq_copy(step).start()
+
+    for kind in range(2):
+        for step in range(1, cols):
+            far_copy(step, kind).wait_recv()
+            for hop in range(1, subs):
+                near_copy(step, hop, kind).start()
+    for copy in locals_:
+        copy.wait()
+    for step in range(1, strips):
+        mod_copy(step).wait_recv()
+    for kind in range(2):
+        for step in range(cols):
+            for hop in range(1, subs):
+                near_copy(step, hop, kind).wait_recv()
+    seq_local.wait()
+
+    @pl.loop(0, strips)
+    def _(turn):
+        there = lax.rem(row + strips - turn, strips)
+
+        @pl.loop(0, group)
+        def _(member):
+            @pl.when(turn * group + member > 0)
+            def _():
+                seq_copy(turn * group + member).wait_recv()
+
+        @pl.loop(0, share)
+        def _(index):
+            slot = there * share + index
+            values = [tokens[g, slot].astype(jnp.float32) for g in range(group)]
+            rows = mods[there]
+            pieces = attend_slot(values, rows[0:1, :full], rows[0:1, full:], proj, weight)
+            for g, piece in enumerate(pieces):
+                done[g, slot] = piece
+
+        @pl.loop(0, group)
+        def _(member):
+            step = turn * group + member
+
+            @pl.when(step > 0)
+            def _():
+                back_copy(step).start()
+
+            @pl.when(step == 0)
+            def _():
+                back_local.start()
+
+    for kind in range(2):
+        for step in range(1, cols):
+            far_copy(step, kind).wait_send()
+        for step in range(cols):
+            for hop in range(1, subs):
+                near_copy(step, hop, kind).wait_send()
+    for step in range(1, strips):
+        mod_copy(step).wait_send()
+    back_local.wait()
+
+    @pl.loop(1, total)
+    def _(step):
+        seq_copy(step).wait_send()
+        back_copy(step).wait()
+
+
+def travel(sequence, modulation, projection, out_weight, cols, subs):
+    strips, per_owner, tokens, width = sequence.shape
+    group = cols * subs
+    slots = strips * per_owner // group
+    total = strips * group
+    sems = pltpu.SemaphoreType.DMA
+    return pl.pallas_call(
+        functools.partial(travel_kernel, strips, cols, subs),
+        out_shape=jax.ShapeDtypeStruct((strips, per_owner, TILE, width), jnp.bfloat16),
+        in_specs=[pl.BlockSpec(memory_space=pl.ANY)] * 4,
+        out_specs=pl.BlockSpec(memory_space=pl.ANY),
+        scratch_shapes=[
+            pltpu.VMEM((group, slots, tokens, width), jnp.bfloat16),
+            pltpu.VMEM((strips,) + modulation.shape, jnp.float32),
+            pltpu.VMEM((group,) + projection.shape, jnp.bfloat16),
+            pltpu.VMEM((group,) + out_weight.shape, jnp.bfloat16),
+            pltpu.VMEM((group, slots, TILE, width), jnp.bfloat16),
+            sems((total,)),
+            sems((total,)),
+            sems((total,)),
+            sems((total,)),
+            sems((strips,)),
+            sems((strips,)),
+            sems((2 * cols,)),
+            sems((2 * cols,)),
+            sems((2 * group,)),
+            sems((2 * group,)),
+            sems((5,)),
+        ],
+        compiler_params=pltpu.CompilerParams(
+            collective_id=0, has_side_effects=True, vmem_limit_bytes=40 * 1024 * 1024
+        ),
+        name="travel",
+    )(sequence, modulation, projection, out_weight)
 
 
 def attend(inputs, scale, shift, projection, out_weight):
@@ -251,28 +484,43 @@
     outgoing = sequence.reshape(strips, per_owner, 2 * TILE, channels)
     group_size = lax.axis_size(("col", "sub"))
     my_slots = tile_count // group_size
-    arrived = lax.all_to_all(outgoing, "row", split_axis=0, concat_axis=0, tiled=True)
-    arrived = arrived.reshape(group_size, my_slots, 2 * TILE, channels)
-    gathered_bands = lax.all_gather(coarse_bands, "row", axis=0, tiled=True)
-    band_means = jnp.mean(gathered_bands.astype(jnp.float32), axis=2)
-    modulation = jnp.dot(
-        band_means, band_weight.astype(jnp.float32), precision=lax.Precision.HIGHEST
-    ) + step_embedding(noise_step, band_weight.shape[1])
     full_width = band_weight.shape[1] // 2
-    inputs = lax.all_to_all(arrived, ("col", "sub"), split_axis=0, concat_axis=0, tiled=True)
-    full_proj = lax.all_gather(
-        jnp.transpose(expert_projections[0], (1, 0, 2)), ("col", "sub"), axis=0, tiled=False
-    )
-    full_out = lax.all_gather(expert_output[0], ("col", "sub"), axis=0, tiled=False)
-    local_mod = pick_rows(
-        modulation, lax.axis_index(("col", "sub")) * my_slots, my_slots, per_owner
-    )
-    heads_out = attend(
-        inputs, local_mod[:, :full_width], local_mod[:, full_width:], full_proj, full_out
-    )
-    returned = lax.all_to_all(heads_out, ("col", "sub"), split_axis=0, concat_axis=0, tiled=True)
-    returned = returned.reshape(strips, per_owner, TILE, channels)
-    results = lax.all_to_all(returned, "row", split_axis=0, concat_axis=0, tiled=True)
+    own_proj = jnp.transpose(expert_projections[0], (1, 0, 2))
+    if per_owner % group_size == 0:
+        own_means = jnp.mean(coarse_bands.astype(jnp.float32), axis=2)
+        own_mod = jnp.dot(
+            own_means, band_weight.astype(jnp.float32), precision=lax.Precision.HIGHEST
+        ) + step_embedding(noise_step, band_weight.shape[1])
+        results = travel(
+            outgoing,
+            jnp.broadcast_to(own_mod, (8, band_weight.shape[1])),
+            own_proj,
+            expert_output[0],
+            lax.axis_size("col"),
+            lax.axis_size("sub"),
+        )
+    else:
+        arrived = lax.all_to_all(outgoing, "row", split_axis=0, concat_axis=0, tiled=True)
+        arrived = arrived.reshape(group_size, my_slots, 2 * TILE, channels)
+        gathered_bands = lax.all_gather(coarse_bands, "row", axis=0, tiled=True)
+        band_means = jnp.mean(gathered_bands.astype(jnp.float32), axis=2)
+        modulation = jnp.dot(
+            band_means, band_weight.astype(jnp.float32), precision=lax.Precision.HIGHEST
+        ) + step_embedding(noise_step, band_weight.shape[1])
+        inputs = lax.all_to_all(arrived, ("col", "sub"), split_axis=0, concat_axis=0, tiled=True)
+        full_proj = lax.all_gather(
+            own_proj, ("col", "sub"), axis=0, tiled=False
+        )
+        full_out = lax.all_gather(expert_output[0], ("col", "sub"), axis=0, tiled=False)
+        local_mod = pick_rows(
+            modulation, lax.axis_index(("col", "sub")) * my_slots, my_slots, per_owner
+        )
+        heads_out = attend(
+            inputs, local_mod[:, :full_width], local_mod[:, full_width:], full_proj, full_out
+        )
+        returned = lax.all_to_all(heads_out, ("col", "sub"), split_axis=0, concat_axis=0, tiled=True)
+        returned = returned.reshape(strips, per_owner, TILE, channels)
+        results = lax.all_to_all(returned, "row", split_axis=0, concat_axis=0, tiled=True)
     results = results.reshape(tile_count, TILE, channels)
     return merge_tiles(
         smoothed, results, jnp.minimum(slot_of, tile_count - 1), land_flat, tile_order

time: 320 us -> 197 us (0.62)
  blocking collectives: 190 us -> 0 us
  Pallas kernels: 54.6 us -> 173 us
  waiting for transfers between devices: 35.2 us -> 2.12 us
  between operations: 14.3 us -> 0.84 us
  starting transfers between devices: 11.9 us -> 6.24 us
    all_to_all x3 -> x0, blocking collectives: 177 us -> none  [the longest x1 97.8 us: body(): lax.all_to_all(outgoing, 'row', split_axis=0, concat_axis=0, tiled=True)]
    pallas_call x1, Pallas kernels: 40.1 us -> 158 us  [travel(): pl.pallas_call(functools.partial(travel_kernel, strips, cols, subs), out_...]
    all_to_all x1 -> x0, waiting for transfers between devices: 33.7 us -> none  [body(): lax.all_to_all(arrived, ('col', 'sub'), split_axis=0, concat_axis=0, tile...]
    all_gather x1 -> x0, blocking collectives: 13.1 us -> none  [body(): gathered_bands = lax.all_gather(coarse_bands, 'row', axis=0, tiled=True)]
    all_to_all x1 -> x0, starting transfers between devices: 4.98 us -> none  [body(): lax.all_to_all(arrived, ('col', 'sub'), split_axis=0, concat_axis=0, tile...]
  transfers between devices with their start and end apart: 5 -> 2, of which waited for: 2 -> 1; matrix products, arithmetic and copies ran while one was open for 4% -> 3% of each run, Pallas kernels for 3% -> 0%
where the time goes in v3:
time: 197 us; the launch traced here: 195 us
  Pallas kernels  173 us (88%)
  other arithmetic  9.18 us (5%)
  starting transfers between devices  6.24 us (3%)
  local copies, waits for them, and re-layouts  3.89 us (2%)
  waiting for transfers between devices  2.12 us (1%)
    pallas_call x1, Pallas kernels, travel(): pl.pallas_call(functools.partial(travel_kernel, strips, cols, subs), out_...  158 us
    pallas_call x1, Pallas kernels, gather_tiles(): pl.pallas_call(gather_kernel, grid_spec=pltpu.PrefetchScalarGridSpec(num_...  9.99 us
    ppermute x1, starting transfers between devices, extended(): lax.ppermute(tail, axis, [(i, (i + 1) % count) for i in range(ends)])  4.94 us
    pallas_call x1, Pallas kernels, merge_tiles(): pl.pallas_call(functools.partial(merge_kernel, tiles_row), grid_spec=pltp...  4.51 us
    convert_element_type x1, other arithmetic, body(): smoothed = running.astype(jnp.bfloat16)  4.34 us
  transfers between devices with their start and end apart: 2, of which 1 were waited for; matrix products, arithmetic and copies ran while one was open for 3% of the time, Pallas kernels for 0%

profile of v3, /device:TPU:0, one launch (start us, length us, event | category | flops | bytes accessed | tf_op | source)
XLA Modules:
  0.0 195.4 jit_solution(6471629464184676800)
XLA Ops:
  0.0 1.2 fusion.23
  1.2 4.9 %collective-permute-start = (bf16[1,512,256]{2,1,0:T(8,128)(2,1)S(1)}, bf16[1,512,256]{2,1,0:T(8,128)(2,1)S(1)}, u32[]{:S(2)}, u32[]{:S(2)}) collective-permute-start(bf16[1,512,256]{2,1,0:T(8,128)(2,1)S(1)} %get-tuple-element.7), channel_id=1, source_target_pairs={{0,4},{4,8},{8,12},{1,5},{5,9},{9,13},{2,6},{6,10},{10,14},{3,7},{... | collective-permute-start | bytes 786440 | tf_op jit(solution)/shard_map/ppermute | solution.py:26
  6.2 1.3 collective-permute-start.1
  7.5 0.8 convert_reduce_fusion
  8.3 0.8 copy.25
  9.1 0.1 broadcast_in_dim_reshape.2.land_ref
  9.2 0.8 copy.24
  9.9 0.1 reshape.55
  10.0 0.2 convert_reduce_fusion.1
  10.2 0.9 fusion.24
  11.1 0.2 fusion.18
  11.2 0.8 broadcast_add_fusion
  12.0 0.7 pad_add_fusion
  12.8 0.1 select_reduce_fusion.tile_ref
  13.5 0.1 copy.26
  13.6 0.1 multiply_add_fusion
  13.7 2.1 %collective-permute-done.1 = bf16[1,512,256]{2,1,0:T(8,128)(2,1)S(1)} collective-permute-done((bf16[1,512,256]{2,1,0:T(8,128)(2,1)S(1)}, bf16[1,512,256]{2,1,0:T(8,128)(2,1)S(1)}, u32[]{:S(2)}, u32[]{:S(2)}) %collective-permute-start.1) | collective-permute-done | bytes 262176 | tf_op jit(solution)/shard_map/ppermute | solution.py:28
  15.8 2.1 %fusion.14 = bf16[10,514,256]{2,1,0:T(8,128)(2,1)S(1)} fusion(bf16[1,512,256]{2,1,0:T(8,128)(2,1)S(1)} %collective-permute-done.1, bf16[8,512,256]{2,1,0:T(8,128)(2,1)} %param.12, bf16[1,512,256]{2,1,0:T(8,128)(2,1)S(1)} %collective-permute-done), kind=kLoop, calls=%fused_computation.18 | loop fusion | flops 15790080 | bytes 5253120 | tf_op jit(solution)/shard_map/concatenate | solution.py:24
  18.0 0.0 copy-start.4
  18.0 4.3 %fusion.9.field_ref = bf16[8,512,256]{2,1,0:T(8,128)(2,1)S(1)} fusion(bf16[8,512,256]{2,1,0:T(8,128)(2,1)S(1)} %copy-done.5, bf16[10,514,256]{2,1,0:T(8,128)(2,1)S(1)} %fusion.14, bf16[1,512,256]{2,1,0:T(8,128)(2,1)S(1)} %collective-permute-done.1, bf16[1,512,256]{2,1,0:T(8,128)(2,1)S(1)} %collective-permute-done, f32[256]{0:T(256)S(1)} %bitcast.43, ...), kind=kLoop, calls=%fused_computation.13 | loop fusion | flops 31457280 | bytes 17310720 | tf_op jit(solution)/shard_map/convert_element_type | solution.py:462
  22.3 0.0 copy-start.1
  22.4 10.0 %gather_tiles.1 = bf16[32,256,256]{2,1,0:T(8,128)(2,1)S(1)} custom-call(s32[32]{0:T(128)S(1)} %select_reduce_fusion.tile_ref, bf16[8,512,256]{2,1,0:T(8,128)(2,1)S(1)} %fusion.9.field_ref, s32[256,32]{1,0:T(8,128)S(1)} %bitcast.31, bf16[256,256]{1,0:T(8,128)(2,1)S(1)} %copy-done.4), custom_call_target="tpu_custom_call" | custom-call | flops 2147483648 | bytes 12582912 | tf_op jit(solution)/shard_map/gather_tiles/pallas_call | solution.py:56
  32.4 158.5 %travel.1 = bf16[4,8,128,256]{3,2,1,0:T(8,128)(2,1)S(1)} custom-call(bf16[4,8,256,256]{3,2,1,0:T(8,128)(2,1)S(1)} %bitcast.28, f32[8,2048]{1,0:T(8,128)S(1)} %broadcast_in_dim.2.mod_ref, bf16[3,1024,256]{2,1,0:T(8,128)(2,1)S(1)} %bitcast.29, bf16[256,1024]{1,0:T(8,128)(2,1)S(1)} %bitcast.30), custom_call_target="tpu_custom_call" | custom-call | tf_op jit(solution)/shard_map/travel/pallas_call | solution.py:370
  190.9 4.5 %merge_tiles.1 = bf16[8,512,256]{2,1,0:T(8,128)(2,1)} custom-call(s32[32]{0:T(128)S(1)} %get-tuple-element.5.slot_ref, s32[32]{0:T(128)S(1)} %broadcast_in_dim_reshape.2.land_ref, bf16[8,512,256]{2,1,0:T(8,128)(2,1)S(1)} %fusion.9.field_ref, s32[8,4,128]{2,1,0:T(4,128)S(1)} %copy-done.3, bf16[32,128,256]{2,1,0:T(8,128)(2,1)S(1)} %bitcast.24, ...), custom_call_target="tpu_custom_call" | custom-call | tf_op jit(solution)/shard_map/merge_tiles/pallas_call | solution.py:102
  (15 shorter events, 0.1 us)
Async XLA Ops:
  0.0 11.0 %copy-start = (bf16[34,2048]{1,0:T(8,128)(2,1)S(1)}, bf16[34,2048]{1,0:T(8,128)(2,1)}, u32[]{:S(2)}) copy-start(bf16[34,2048]{1,0:T(8,128)(2,1)} %param.16) | copy-start | bytes 417796
  0.0 18.0 %copy-start.5 = (bf16[8,512,256]{2,1,0:T(8,128)(2,1)S(1)}, bf16[8,512,256]{2,1,0:T(8,128)(2,1)}, u32[]{:S(2)}) copy-start(bf16[8,512,256]{2,1,0:T(8,128)(2,1)} %param.12) | copy-start | bytes 6291460
  1.2 12.5 %collective-permute-start = (bf16[1,512,256]{2,1,0:T(8,128)(2,1)S(1)}, bf16[1,512,256]{2,1,0:T(8,128)(2,1)S(1)}, u32[]{:S(2)}, u32[]{:S(2)}) collective-permute-start(bf16[1,512,256]{2,1,0:T(8,128)(2,1)S(1)} %get-tuple-element.7), channel_id=1, source_target_pairs={{0,4},{4,8},{8,12},{1,5},{5,9},{9,13},{2,6},{6,10},{10,14},{3,7},{... | collective-permute-start | bytes 786440 | tf_op jit(solution)/shard_map/ppermute | solution.py:26
  6.2 9.7 %collective-permute-start.1 = (bf16[1,512,256]{2,1,0:T(8,128)(2,1)S(1)}, bf16[1,512,256]{2,1,0:T(8,128)(2,1)S(1)}, u32[]{:S(2)}, u32[]{:S(2)}) collective-permute-start(bf16[1,512,256]{2,1,0:T(8,128)(2,1)S(1)} %get-tuple-element.8), channel_id=1, source_target_pairs={{4,0},{8,4},{12,8},{5,1},{9,5},{13,9},{6,2},{10,6},{14,10},{7,3},{... | collective-permute-start | bytes 786440 | tf_op jit(solution)/shard_map/ppermute | solution.py:28
  18.0 4.4 %copy-start.4 = (bf16[256,256]{1,0:T(8,128)(2,1)S(1)}, bf16[256,256]{1,0:T(8,128)(2,1)}, u32[]{:S(2)}) copy-start(bf16[256,256]{1,0:T(8,128)(2,1)} %table_ref.1) | copy-start | bytes 393220
  22.3 10.1 %copy-start.1 = (bf16[1,1024,3,256]{3,1,2,0:T(8,128)(2,1)S(1)}, bf16[1,1024,3,256]{3,1,2,0:T(8,128)(2,1)}, u32[]{:S(2)}) copy-start(bf16[1,1024,3,256]{3,1,2,0:T(8,128)(2,1)} %param.22) | copy-start | bytes 4718596
  22.4 10.1 %copy-start.2 = (bf16[1,256,1024]{2,1,0:T(8,128)(2,1)S(1)}, bf16[1,256,1024]{2,1,0:T(8,128)(2,1)}, u32[]{:S(2)}) copy-start(bf16[1,256,1024]{2,1,0:T(8,128)(2,1)} %param.23) | copy-start | bytes 1572868
  32.4 158.5 %copy-start.3 = (s32[8,4,128]{2,1,0:T(4,128)S(1)}, s32[8,4,128]{2,1,0:T(4,128)}, u32[]{:S(2)}) copy-start(s32[8,4,128]{2,1,0:T(4,128)} %order_ref.1) | copy-start | bytes 49156
